TPU v7x, 32 devices: a whole 2x2x4 slice. The times are simulated.
32 devices in a mesh: row: 2 (over x), col: 4 (over z), depth: 4 (over y, core).
Axes of the slice: x: 2, y: 2, z: 4, core: 2. Of those that a mesh axis runs over, the one named last changes fastest.
Arguments:
- tokens: bfloat16 [512, 4096], P(('col', 'depth'), 'row'), may hold values from -72 to 72
- norm_gain: float32 [4096], P('row'), may hold values from 0.25 to 1.75
- w_gate: bfloat16 [4096, 14336], P('row', 'col'), may hold values from -0.09375 to 0.09375
- w_up: bfloat16 [4096, 14336], P('row', 'col'), may hold values from -0.09375 to 0.09375
- w_down: bfloat16 [14336, 4096], P('col', 'row'), may hold values from -0.046875 to 0.046875
- cotangent: bfloat16 [512, 4096], P(('col', 'depth'), 'row'), may hold values from -1.5 to 1.5
Outputs:
- output: bfloat16 [512, 4096], P(('col', 'depth'), 'row')
- grad_tokens: bfloat16 [512, 4096], P(('col', 'depth'), 'row')
- grad_gain: float32 [4096], P('row')
- grad_gate: bfloat16 [4096, 14336], P('row', 'col')
- grad_up: bfloat16 [4096, 14336], P('row', 'col')
- grad_down: bfloat16 [14336, 4096], P('col', 'row')
All inputs are finite; a program needn't handle non-finite values.
Results may differ from a plain program's by a relative error of at most 0.023.
Values may be sent and summed in bfloat16 or wider, within the bound.
A program may use at most 192 MiB of HBM per device.

v0:
```python
import jax
import jax.numpy as jnp
from jax import lax
from jax.sharding import PartitionSpec as P

D = 4096


EPS = 1e-05


def contract_rows(left, right):
    return lax.dot_general(
        left, right, (((0,), (0,)), ((), ())), preferred_element_type=jnp.float32
    )


def contract_cols(left, right):
    return lax.dot_general(
        left, right, (((1,), (1,)), ((), ())), preferred_element_type=jnp.float32
    )


def body(tokens, norm_gain, w_gate, w_up, w_down, cotangent):
    inputs = tokens.astype(jnp.float32)
    sumsq = lax.psum(jnp.sum(inputs * inputs, axis=1), "row")
    inv_rms = lax.rsqrt(sumsq / D + EPS)[:, None]
    normal_rows = inputs * inv_rms
    normed = (normal_rows * norm_gain[None, :]).astype(jnp.bfloat16)
    gathered = lax.all_gather(normed, "col", axis=0, tiled=True)
    hidden_cols = w_gate.shape[1]
    piece = gathered
    joined = lax.psum_scatter(
        jnp.concatenate(
            [
                jnp.dot(piece, w_gate, preferred_element_type=jnp.float32),
                jnp.dot(piece, w_up, preferred_element_type=jnp.float32),
            ],
            axis=1,
        ).astype(jnp.bfloat16),
        "row",
        scatter_dimension=0,
        tiled=True,
    ).astype(jnp.float32)
    gate = joined[:, :hidden_cols]
    up = joined[:, hidden_cols:]
    sig = jax.nn.sigmoid(gate)
    act = gate * sig
    hidden = (act * up).astype(jnp.bfloat16)
    hidden_all = lax.all_gather(hidden, "row", axis=0, tiled=True)
    piece = hidden_all
    mixed = lax.psum_scatter(
        jnp.dot(piece, w_down, preferred_element_type=jnp.float32).astype(jnp.bfloat16),
        "col",
        scatter_dimension=0,
        tiled=True,
    ).astype(jnp.float32)
    output = (inputs + mixed).astype(jnp.bfloat16)
    cot_all = lax.all_gather(cotangent, "col", axis=0, tiled=True)
    piece = cot_all
    grad_hidden = lax.psum_scatter(
        contract_cols(piece, w_down).astype(jnp.bfloat16), "row", scatter_dimension=0, tiled=True
    ).astype(jnp.float32)
    down_grad = contract_rows(hidden_all, cot_all)
    down_sum = lax.psum(down_grad.astype(jnp.bfloat16), "depth")
    grad_up_h = (grad_hidden * act).astype(jnp.bfloat16)
    grad_gate_h = (grad_hidden * up * sig * (1.0 + gate * (1.0 - sig))).astype(jnp.bfloat16)
    gate_all, up_all = (
        lax.all_gather(grad_gate_h, "row", axis=0, tiled=True),
        lax.all_gather(grad_up_h, "row", axis=0, tiled=True),
    )
    gate_grad = contract_rows(gathered, gate_all)
    up_grad = contract_rows(gathered, up_all)
    grad_normed = lax.psum_scatter(
        (contract_cols(gate_all, w_gate) + contract_cols(up_all, w_up)).astype(jnp.bfloat16),
        "col",
        scatter_dimension=0,
        tiled=True,
    ).astype(jnp.float32)
    grad_scaled = grad_normed * norm_gain[None, :]
    proj = lax.psum(jnp.sum(grad_scaled * normal_rows, axis=1), "row")
    grad_tokens = (
        cotangent.astype(jnp.float32) + inv_rms * (grad_scaled - normal_rows * (proj / D)[:, None])
    ).astype(jnp.bfloat16)
    grad_gain = lax.psum(jnp.sum(grad_normed * normal_rows, axis=0), ("col", "depth"))
    gate_sum, up_sum = (
        lax.psum(gate_grad.astype(jnp.bfloat16), "depth").astype(jnp.float32),
        lax.psum(up_grad.astype(jnp.bfloat16), "depth").astype(jnp.float32),
    )
    return (
        output,
        grad_tokens,
        grad_gain,
        gate_sum.astype(jnp.bfloat16),
        up_sum.astype(jnp.bfloat16),
        down_sum,
    )


def solution(mesh):
    in_specs = (
        P(("col", "depth"), "row"),
        P("row"),
        P("row", "col"),
        P("row", "col"),
        P("col", "row"),
        P(("col", "depth"), "row"),
    )
    out_specs = (
        P(("col", "depth"), "row"),
        P(("col", "depth"), "row"),
        P("row"),
        P("row", "col"),
        P("row", "col"),
        P("col", "row"),
    )
    return jax.shard_map(body, mesh=mesh, in_specs=in_specs, out_specs=out_specs, check_vma=False)
```

profile of v0, /device:TPU:0, one launch (start us, length us, event | category | flops | bytes accessed | tf_op | source)
XLA Modules:
  0.0 980.3 jit_solution(6682877606259504175)
XLA Ops:
  7.2 1.0 fusion.17
  8.2 5.8 psum.42
  14.1 1.2 fusion.14
  15.3 15.8 %all_gather.15 = bf16[128,2048]{1,0:T(8,128)(2,1)S(1)} all-gather(bf16[32,2048]{1,0:T(8,128)(2,1)S(1)} %fusion.14), channel_id=1, replica_groups=mesh['row'=2,'col'=4,'depth'=4] {'col'}, dimensions={0}, use_global_device_ids=true | all-gather | bytes 655360 | tf_op jit(solution)/shard_map/all_gather | solution.py:30
  31.1 7.3 convolution_convert_fusion.4
  38.4 2.2 convolution_convert_fusion.5
  40.6 1.4 pad_maximum_fusion
  42.0 15.9 %all_gather.17 = bf16[128,2048]{1,0:T(8,128)(2,1)S(1)} all-gather(bf16[32,2048]{1,0:T(8,128)(2,1)S(1)} %copy-done.3), channel_id=1, replica_groups=mesh['row'=2,'col'=4,'depth'=4] {'col'}, dimensions={0}, use_global_device_ids=true | all-gather | bytes 655360 | tf_op jit(solution)/shard_map/all_gather | solution.py:59
  58.0 11.1 %convolution_convert_fusion.3 = bf16[128,3584]{1,0:T(8,128)(2,1)} fusion(bf16[128,2048]{1,0:T(8,128)(2,1)S(1)} %all_gather.17, bf16[3584,2048]{1,0:T(8,128)(2,1)} %param.10), kind=kOutput, calls=%fused_computation.3 | convolution fusion | flops 1879506944 | bytes 16121856 | tf_op jit(solution)/shard_map/dot_general | solution.py:19
  69.1 3.5 reduce-scatter.5.cloned.1.call-done
  72.6 1.3 convert_element_type.61
  73.9 20.5 %reduce-scatter.9.cloned.1.call-done = bf16[64,3584]{1,0:T(8,128)(2,1)} async-done(((bf16[128,3584]{1,0:T(8,128)(2,1)}), bf16[64,3584]{1,0:T(8,128)(2,1)}) %reduce-scatter.9.cloned.1.call-update) | async-done | bytes 458768 | tf_op jit(solution)/shard_map/reduce_scatter | solution.py:61
  94.4 2.3 fusion.4
  96.7 13.1 %all_gather.16 = bf16[128,3584]{1,0:T(8,128)(2,1)S(1)} all-gather(bf16[64,3584]{1,0:T(8,128)(2,1)S(1)} %get-tuple-element.13), channel_id=1, replica_groups=mesh['row'=2,'col'=4,'depth'=4] {'row'}, dimensions={0}, use_global_device_ids=true | all-gather | bytes 1376256 | tf_op jit(solution)/shard_map/all_gather | solution.py:50
  109.8 8.0 convolution_convert_fusion.6
  117.8 7.6 convolution_convert_fusion
  125.4 12.3 %all_gather.19 = bf16[128,3584]{1,0:T(8,128)(2,1)S(1)} all-gather(bf16[64,3584]{1,0:T(8,128)(2,1)} %get-tuple-element.11), channel_id=1, replica_groups=mesh['row'=2,'col'=4,'depth'=4] {'row'}, dimensions={0}, use_global_device_ids=true | all-gather | bytes 1376256 | tf_op jit(solution)/shard_map/all_gather | solution.py:70
  137.7 11.1 %all_gather.18 = bf16[128,3584]{1,0:T(8,128)(2,1)S(1)} all-gather(bf16[64,3584]{1,0:T(8,128)(2,1)S(1)} %get-tuple-element.12), channel_id=1, replica_groups=mesh['row'=2,'col'=4,'depth'=4] {'row'}, dimensions={0}, use_global_device_ids=true | all-gather | bytes 1376256 | tf_op jit(solution)/shard_map/all_gather | solution.py:69
  148.8 9.9 %fusion.19 = f32[128,2048]{1,0:T(8,128)S(1)} fusion(bf16[128,3584]{1,0:T(8,128)(2,1)S(1)} %all_gather.18, bf16[2048,3584]{1,0:T(8,128)(2,1)} %param.8), kind=kOutput, calls=%fused_computation.38 | convolution fusion | flops 1879048192 | bytes 16646144 | tf_op jit(solution)/shard_map/dot_general | solution.py:19
  158.7 10.7 %fusion = bf16[128,2048]{1,0:T(8,128)(2,1)} fusion(f32[128,2048]{1,0:T(8,128)S(1)} %fusion.19, bf16[128,3584]{1,0:T(8,128)(2,1)S(1)} %all_gather.19, bf16[2048,3584]{1,0:T(8,128)(2,1)} %param.9), kind=kOutput, calls=%fused_computation.7 | convolution fusion | flops 1879572480 | bytes 17170432 | tf_op jit(solution)/shard_map/dot_general | solution.py:19
  169.5 7.6 convolution_convert_fusion.1
  177.4 7.6 convolution_convert_fusion.2
  185.0 6.2 reduce-scatter.11.cloned.1.call-done
  191.3 1.2 fusion.16
  192.4 4.9 psum.43
  197.4 31.0 %psum.44 = f32[2048]{0:T(1024)} all-reduce(f32[2048]{0:T(1024)S(1)} %get-tuple-element.6), channel_id=1, replica_groups=mesh['row'=2,'col'=4,'depth'=4] {'col','depth'}, use_global_device_ids=true, to_apply=%region_9.0 | all-reduce | flops 2048 | bytes 16384 | tf_op jit(solution)/shard_map/psum | solution.py:85
  228.4 1.8 fusion.13
  230.1 713.6 %all-reduce.3.cloned.1.call-done = (bf16[2048,3584]{1,0:T(8,128)(2,1)}, bf16[2048,3584]{1,0:T(8,128)(2,1)}, bf16[3584,2048]{1,0:T(8,128)(2,1)}) async-done(((bf16[2048,3584]{1,0:T(8,128)(2,1)}, bf16[2048,3584]{1,0:T(8,128)(2,1)}, bf16[3584,2048]{1,0:T(8,128)(2,1)}), (bf16[2048,3584]{1,0:T(8,128)(2,1)}, bf16[2048,3584]{1,0:T(8,128)(2,1)}, bf16[3584,2048]{1,0:T(8,128)(2,1)})) %all-reduce.3.cloned.1.call-update) | async-done | bytes 44040208 | tf_op jit(solution)/shard_map/psum | solution.py:87
  943.7 15.7 %copy.15 = bf16[2048,3584]{1,0:T(8,128)(2,1)} copy(bf16[2048,3584]{1,0:T(8,128)(2,1)} %get-tuple-element.19) | data formatting | bytes 29360128
  959.5 7.4 copy.16
  967.0 1.3 slice-done.3
  968.4 5.5 copy.17
  (31 shorter events, 0.7 us)
Async XLA Ops:
  7.2 65.4 %reduce-scatter.5.cloned.1.call-start = ((), (), s32[]{:S(2)}) async-start(), calls=%async_computation.4 | async-start | bytes 2752512 | tf_op jit(solution)/shard_map/reduce_scatter | solution.py:33
  14.1 24.3 %copy-start = (bf16[2048,3584]{1,0:T(8,128)(2,1)S(1)}, bf16[2048,3584]{1,0:T(8,128)(2,1)}, u32[]{:S(2)}) copy-start(bf16[2048,3584]{1,0:T(8,128)(2,1)} %param.8) | copy-start | bytes 44040196
  38.4 3.7 copy-start.3
  42.0 52.4 %reduce-scatter.9.cloned.1.call-start = ((), (), s32[]{:S(2)}) async-start(), calls=%async_computation.6 | async-start | bytes 1376256 | tf_op jit(solution)/shard_map/reduce_scatter | solution.py:61
  69.1 122.2 %reduce-scatter.11.cloned.1.call-start = ((), (), s32[]{:S(2)}) async-start(), calls=%async_computation.7 | async-start | bytes 655360 | tf_op jit(solution)/shard_map/reduce_scatter | solution.py:74
  169.5 58.9 %reduce-scatter.7.cloned.1.call-start = ((), (), s32[]{:S(2)}) async-start(), calls=%async_computation.5 | async-start | bytes 655360 | tf_op jit(solution)/shard_map/reduce_scatter | solution.py:52
  177.1 766.6 %all-reduce.3.cloned.1.call-start = ((), (), s32[]{:S(2)}) async-start(), calls=%async_computation.8 | async-start | bytes 88080384 | tf_op jit(solution)/shard_map/psum | solution.py:87
  185.0 6.3 copy-start.2
  185.0 6.3 copy-start.4
  943.7 15.7 %copy-start.1 = (bf16[2048,3584]{1,0:T(8,128)(2,1)S(1)}, bf16[2048,3584]{1,0:T(8,128)(2,1)}, u32[]{:S(2)}) copy-start(bf16[2048,3584]{1,0:T(8,128)(2,1)} %get-tuple-element.20) | copy-start | bytes 44040196
  943.7 23.2 %slice-start = ((s8[14680064]{0:T(1024)(128)(4,1)}), s8[4194304]{0:T(1024)(128)(4,1)S(1)}, s32[]{:S(2)}) async-start(s8[14680064]{0:T(1024)(128)(4,1)} %bitcast.18), calls=%async_computation.9 | async-start | bytes 8388608
  943.7 23.2 %slice-start.1 = ((s8[14680064]{0:T(1024)(128)(4,1)}), s8[4194304]{0:T(1024)(128)(4,1)S(1)}, s32[]{:S(2)}) async-start(s8[14680064]{0:T(1024)(128)(4,1)} %bitcast.18), calls=%async_computation.10 | async-start | bytes 8388608
  959.5 7.6 slice-start.2
  959.5 8.9 slice-start.3
Sparse Core Ops, SparseCore 0:
  42.1 30.4 reduce-scatter.4
  75.5 18.8 reduce-scatter.8
  169.6 21.6 reduce-scatter.10
  193.4 19.9 reduce-scatter.6
  216.7 727.0 all-reduce.2
where the time goes:
time: 981 us; the launch traced here: 980 us
  waiting for transfers between devices  744 us (76%)
  blocking collectives  110 us (11%)
  matrix products  71.9 us (7%)
  local copies, waits for them, and re-layouts  30.1 us (3%)
  between operations  13.8 us (1%)
  other arithmetic  10.1 us (1%)
    psum x1, waiting for transfers between devices, body(): lax.psum(gate_grad.astype(jnp.bfloat16), 'depth').astype(jnp.float32)  714 us
    dot_general x3, matrix products, contract_cols(): lax.dot_general(left, right, (((1,), (1,)), ((), ())), preferred_element_...  31.7 us
    psum x1, blocking collectives, body(): lax.psum(jnp.sum(grad_normed * normal_rows, axis=0), ('col', 'depth'))  31 us
    unnamed x21, local copies, waits for them, and re-layouts  30.1 us
    dot_general x3, matrix products, contract_rows(): lax.dot_general(left, right, (((0,), (0,)), ((), ())), preferred_element_...  22.7 us
    reduce_scatter x1, waiting for transfers between devices, body(): lax.psum_scatter(contract_cols(piece, w_down).astype(jnp.bfloat16), 'row'...  20.5 us
  transfers between devices with their start and end apart: 5, of which 4 were waited for; matrix products, arithmetic and copies ran while one was open for 3% of the time, Pallas kernels for 0%

commit v1 on v0

v1 whole, which is shorter than its diff:
```python
import jax
import jax.numpy as jnp
from jax import lax
from jax.sharding import PartitionSpec as P

EPS = 1e-05
BF = jnp.bfloat16
F32 = jnp.float32


def contract_rows(left, right):
    return lax.dot_general(left, right, (((0,), (0,)), ((), ())), preferred_element_type=F32)


def contract_cols(left, right):
    return lax.dot_general(left, right, (((1,), (1,)), ((), ())), preferred_element_type=F32)


def make_body(mesh):
    n_row = mesh.shape["row"]

    def row_total(value):
        if n_row == 2:
            return value.astype(F32) + lax.ppermute(value, "row", [(0, 1), (1, 0)]).astype(F32)
        return lax.psum(value, "row").astype(F32)

    def body(tokens, norm_gain, w_gate, w_up, w_down, cotangent):
        width = tokens.shape[1] * n_row
        inputs = tokens.astype(F32)
        cot_mine = lax.all_gather(cotangent, "col", axis=0, tiled=True)
        sumsq = row_total(jnp.sum(inputs * inputs, axis=1, keepdims=True))
        inv_rms = lax.rsqrt(sumsq / width + EPS)
        normal_rows = inputs * inv_rms
        normed = (normal_rows * norm_gain[None, :]).astype(BF)
        normed_mine = lax.all_gather(normed, "col", axis=0, tiled=True)
        cot_all = lax.all_gather(cot_mine, "depth", axis=0, tiled=True)
        normed_all = lax.all_gather(normed_mine, "depth", axis=0, tiled=True)
        hidden_cols = w_gate.shape[1]
        chunks = 4 if hidden_cols % 512 == 0 else 1
        size = hidden_cols // chunks
        mixed = 0.0
        grad_normed = 0.0
        gates, ups, downs = [], [], []
        parts = []
        for index in range(chunks):
            cols = slice(index * size, (index + 1) * size)
            wg, wu, wd = w_gate[:, cols], w_up[:, cols], w_down[cols, :]
            parts.append(jnp.concatenate(
                [
                    jnp.dot(normed_mine, wg, preferred_element_type=F32).astype(BF),
                    jnp.dot(normed_mine, wu, preferred_element_type=F32).astype(BF),
                    contract_cols(cot_mine, wd).astype(BF),
                ],
                axis=1,
            ))
        trios = []
        for index in range(chunks):
            cols = slice(index * size, (index + 1) * size)
            wg, wu, wd = w_gate[:, cols], w_up[:, cols], w_down[cols, :]
            whole = row_total(parts[index])
            gate, up, grad_hidden = whole[:, :size], whole[:, size:2 * size], whole[:, 2 * size:]
            sig = jax.nn.sigmoid(gate)
            act = gate * sig
            hidden = (act * up).astype(BF)
            grad_up_h = (grad_hidden * act).astype(BF)
            grad_gate_h = (grad_hidden * up * sig * (1.0 + gate * (1.0 - sig))).astype(BF)
            trio = jnp.concatenate([grad_gate_h, grad_up_h, hidden], axis=1)
            trios.append(lax.all_gather(trio, "depth", axis=0, tiled=True))
            mixed = mixed + jnp.dot(hidden, wd, preferred_element_type=F32)
            grad_normed = grad_normed + contract_cols(grad_gate_h, wg) + contract_cols(grad_up_h, wu)
        for trio_all in trios:
            gates.append(contract_rows(normed_all, trio_all[:, :size]).astype(BF))
            ups.append(contract_rows(normed_all, trio_all[:, size:2 * size]).astype(BF))
            downs.append(contract_rows(trio_all[:, 2 * size:], cot_all).astype(BF))
        mixed = lax.psum_scatter(mixed.astype(BF), "col", scatter_dimension=0, tiled=True).astype(F32)
        output = (inputs + mixed).astype(BF)
        grad_normed = lax.psum_scatter(
            grad_normed.astype(BF), "col", scatter_dimension=0, tiled=True
        ).astype(F32)
        grad_scaled = grad_normed * norm_gain[None, :]
        proj = row_total(jnp.sum(grad_scaled * normal_rows, axis=1, keepdims=True))
        grad_tokens = (
            cotangent.astype(F32) + inv_rms * (grad_scaled - normal_rows * (proj / width))
        ).astype(BF)
        grad_gain = lax.psum(jnp.sum(grad_normed * normal_rows, axis=0), ("col", "depth"))
        return (
            output,
            grad_tokens,
            grad_gain,
            jnp.concatenate(gates, axis=1),
            jnp.concatenate(ups, axis=1),
            jnp.concatenate(downs, axis=0),
        )

    return body


def solution(mesh):
    in_specs = (
        P(("col", "depth"), "row"),
        P("row"),
        P("row", "col"),
        P("row", "col"),
        P("col", "row"),
        P(("col", "depth"), "row"),
    )
    out_specs = (
        P(("col", "depth"), "row"),
        P(("col", "depth"), "row"),
        P("row"),
        P("row", "col"),
        P("row", "col"),
        P("col", "row"),
    )
    return jax.shard_map(
        make_body(mesh), mesh=mesh, in_specs=in_specs, out_specs=out_specs, check_vma=False
    )
```

time: 981 us -> 468 us (0.48)
  waiting for transfers between devices: 744 us -> 127 us
  other arithmetic: 10.1 us -> 107 us
  blocking collectives: 110 us -> 63.6 us
  matrix products: 71.9 us -> 101 us
    psum x1 -> x0, waiting for transfers between devices: 714 us -> none  [body(): lax.psum(gate_grad.astype(jnp.bfloat16), 'depth').astype(jnp.float32)]
    concatenate x1 -> x11, other arithmetic: 1.41 us -> 99.2 us  [the longest x1 31.3 us: body(): jnp.concatenate(ups, axis=1)]
    all_gather x0 -> x6, waiting for transfers between devices: none -> 76.5 us  [the longest x4 76.5 us: body(): trios.append(lax.all_gather(trio, 'depth', axis=0, tiled=True))]
    ppermute x0 -> x6, waiting for transfers between devices: none -> 47.3 us  [row_total(): lax.ppermute(value, 'row', [(0, 1), (1, 0)]).astype(F32)]
    all_gather x5 -> x2, blocking collectives: 68.3 us -> 32.4 us  [the longest x1 16.5 us: body(): normed_mine = lax.all_gather(normed, 'col', axis=0, tiled=True)]
    reduce_scatter x4 -> x2, waiting for transfers between devices: 30.2 us -> 2.41 us  [the longest x1 2.4 us: body(): lax.psum_scatter(grad_normed.astype(BF), 'col', scatter_dimension=0, tile...]
    dot_general x3 -> x12, matrix products: 22.7 us -> 46.9 us  [contract_rows(): lax.dot_general(left, right, (((0,), (0,)), ((), ())), preferred_element_...]
    psum x2 -> x0, blocking collectives: 10.8 us -> none  [the longest x1 5.84 us: body(): sumsq = lax.psum(jnp.sum(inputs * inputs, axis=1), 'row')]
  transfers between devices with their start and end apart: 5 -> 14, of which waited for: 4 -> 9; matrix products, arithmetic and copies ran while one was open for 3% -> 37% of each run, Pallas kernels for 0% -> 0%
where the time goes in v1:
time: 468 us; the launch traced here: 463 us
  waiting for transfers between devices  127 us (27%)
  other arithmetic  107 us (23%)
  matrix products  101 us (22%)
  blocking collectives  63.6 us (14%)
  local copies, waits for them, and re-layouts  38.7 us (8%)
  between operations  16.4 us (4%)
  starting transfers between devices  9.11 us (2%)
    all_gather x4, waiting for transfers between devices, body(): trios.append(lax.all_gather(trio, 'depth', axis=0, tiled=True))  76.5 us
    ppermute x6, waiting for transfers between devices, row_total(): lax.ppermute(value, 'row', [(0, 1), (1, 0)]).astype(F32)  47.3 us
    dot_general x12, matrix products, contract_rows(): lax.dot_general(left, right, (((0,), (0,)), ((), ())), preferred_element_...  46.9 us
    unnamed x62, local copies, waits for them, and re-layouts  38.7 us
    concatenate x1, other arithmetic, body(): jnp.concatenate(ups, axis=1)  31.3 us
    concatenate x1, other arithmetic, body(): jnp.concatenate(gates, axis=1)  31.2 us
    psum x1, blocking collectives, body(): lax.psum(jnp.sum(grad_normed * normal_rows, axis=0), ('col', 'depth'))  31.1 us
    concatenate x1, other arithmetic, body(): jnp.concatenate(downs, axis=0)  31.1 us
  transfers between devices with their start and end apart: 14, of which 9 were waited for; matrix products, arithmetic and copies ran while one was open for 37% of the time, Pallas kernels for 0%

profile of v1, /device:TPU:0, one launch (start us, length us, event | category | flops | bytes accessed | tf_op | source)
XLA Modules:
  0.0 462.9 jit_solution(18430014239776099683)
XLA Ops:
  12.1 16.0 %all_gather.25 = bf16[128,2048]{1,0:T(8,128)(2,1)S(1)} all-gather(bf16[32,2048]{1,0:T(8,128)(2,1)} %param.11), channel_id=1, replica_groups=mesh['row'=2,'col'=4,'depth'=4] {'col'}, dimensions={0}, use_global_device_ids=true | all-gather | bytes 655360 | tf_op jit(solution)/shard_map/all_gather | solution.py:30
  28.1 4.2 fusion.117
  32.3 3.3 fusion.108
  35.6 3.3 fusion.99
  38.9 3.5 fusion.90
  42.6 16.5 %all_gather.24 = bf16[128,2048]{1,0:T(8,128)(2,1)S(1)} all-gather(bf16[32,2048]{1,0:T(8,128)(2,1)S(1)} %fusion.144), channel_id=1, replica_groups=mesh['row'=2,'col'=4,'depth'=4] {'col'}, dimensions={0}, use_global_device_ids=true | all-gather | bytes 655360 | tf_op jit(solution)/shard_map/all_gather | solution.py:35
  62.1 3.4 fusion.105
  65.5 3.4 fusion.111
  79.8 13.2 %collective-permute-done.4 = bf16[128,2688]{1,0:T(8,128)(2,1)S(1)} collective-permute-done((bf16[128,2688]{1,0:T(8,128)(2,1)S(1)}, bf16[128,2688]{1,0:T(8,128)(2,1)S(1)}, u32[]{:S(2)}, u32[]{:S(2)}) %collective-permute-start.4) | collective-permute-done | bytes 688160 | tf_op jit(solution)/shard_map/ppermute | solution.py:24
  93.1 14.6 %collective-permute-done.3 = bf16[128,2688]{1,0:T(8,128)(2,1)S(1)} collective-permute-done((bf16[128,2688]{1,0:T(8,128)(2,1)S(1)}, bf16[128,2688]{1,0:T(8,128)(2,1)S(1)}, u32[]{:S(2)}, u32[]{:S(2)}) %collective-permute-start.3) | collective-permute-done | bytes 688160 | tf_op jit(solution)/shard_map/ppermute | solution.py:24
  107.9 14.4 %collective-permute-done.2 = bf16[128,2688]{1,0:T(8,128)(2,1)S(1)} collective-permute-done((bf16[128,2688]{1,0:T(8,128)(2,1)S(1)}, bf16[128,2688]{1,0:T(8,128)(2,1)S(1)}, u32[]{:S(2)}, u32[]{:S(2)}) %collective-permute-start.2) | collective-permute-done | bytes 688160 | tf_op jit(solution)/shard_map/ppermute | solution.py:24
  124.7 5.0 %collective-permute-done.1 = bf16[128,2688]{1,0:T(8,128)(2,1)S(1)} collective-permute-done((bf16[128,2688]{1,0:T(8,128)(2,1)S(1)}, bf16[128,2688]{1,0:T(8,128)(2,1)S(1)}, u32[]{:S(2)}, u32[]{:S(2)}) %collective-permute-start.1) | collective-permute-done | bytes 688160 | tf_op jit(solution)/shard_map/ppermute | solution.py:24
  151.0 3.6 fusion.78
  166.9 31.1 %psum.7 = f32[2048]{0:T(1024)} all-reduce(f32[2048]{0:T(1024)S(1)} %get-tuple-element.12), channel_id=1, replica_groups=mesh['row'=2,'col'=4,'depth'=4] {'col','depth'}, use_global_device_ids=true, to_apply=%region_5.0 | all-reduce | flops 2048 | bytes 16384 | tf_op jit(solution)/shard_map/psum | solution.py:85
  199.8 8.3 %all-gather.9.cloned.1.call-done = bf16[512,2688]{1,0:T(8,128)(2,1)} async-done(((bf16[128,2688]{1,0:T(8,128)(2,1)}), bf16[512,2688]{1,0:T(8,128)(2,1)}) %all-gather.9.cloned.1.call-update) | async-done | bytes 2752528 | tf_op jit(solution)/shard_map/all_gather | solution.py:68
  208.2 5.8 %convolution_convert_fusion.11 = bf16[2048,896]{0,1:T(8,128)(2,1)} fusion(bf16[512,2048]{1,0:T(8,128)(2,1)} %all-gather.7.cloned.1.call-done, bf16[512,2688]{1,0:T(8,128)(2,1)} %all-gather.9.cloned.1.call-done), kind=kOutput, calls=%fused_computation.14 | convolution fusion | flops 1880883200 | bytes 6684672 | tf_op jit(solution)/shard_map/dot_general | solution.py:12
  213.9 22.3 %all-gather.11.cloned.1.call-done = bf16[512,2688]{1,0:T(8,128)(2,1)} async-done(((bf16[128,2688]{1,0:T(8,128)(2,1)}), bf16[512,2688]{1,0:T(8,128)(2,1)}) %all-gather.11.cloned.1.call-update) | async-done | bytes 2752528 | tf_op jit(solution)/shard_map/all_gather | solution.py:68
  236.3 5.1 %convolution_convert_fusion.10 = bf16[2048,896]{0,1:T(8,128)(2,1)} fusion(bf16[512,2048]{1,0:T(8,128)(2,1)S(1)} %copy-done.23, bf16[512,2688]{1,0:T(8,128)(2,1)} %all-gather.11.cloned.1.call-done), kind=kOutput, calls=%fused_computation.13 | convolution fusion | flops 1880883200 | bytes 6684672 | tf_op jit(solution)/shard_map/dot_general | solution.py:12
  241.4 23.2 %all-gather.13.cloned.1.call-done = bf16[512,2688]{1,0:T(8,128)(2,1)} async-done(((bf16[128,2688]{1,0:T(8,128)(2,1)}), bf16[512,2688]{1,0:T(8,128)(2,1)}) %all-gather.13.cloned.1.call-update) | async-done | bytes 2752528 | tf_op jit(solution)/shard_map/all_gather | solution.py:68
  264.6 5.1 %convolution_convert_fusion.9 = bf16[2048,896]{0,1:T(8,128)(2,1)} fusion(bf16[512,2048]{1,0:T(8,128)(2,1)S(1)} %copy-done.23, bf16[512,2688]{1,0:T(8,128)(2,1)} %all-gather.13.cloned.1.call-done), kind=kOutput, calls=%fused_computation.12 | convolution fusion | flops 1880883200 | bytes 6684672 | tf_op jit(solution)/shard_map/dot_general | solution.py:12
  269.7 22.6 %all-gather.15.cloned.1.call-done = bf16[512,2688]{1,0:T(8,128)(2,1)} async-done(((bf16[128,2688]{1,0:T(8,128)(2,1)}), bf16[512,2688]{1,0:T(8,128)(2,1)}) %all-gather.15.cloned.1.call-update) | async-done | bytes 2752528 | tf_op jit(solution)/shard_map/all_gather | solution.py:68
  292.3 3.4 convolution_convert_fusion.8
  296.8 31.2 %pad_maximum_fusion = bf16[2048,3584]{0,1:T(8,128)(2,1)} fusion(bf16[2048,896]{0,1:T(8,128)(2,1)S(1)} %convolution_convert_fusion.8, bf16[2048,896]{0,1:T(8,128)(2,1)S(1)} %copy-done.2, bf16[2048,896]{0,1:T(8,128)(2,1)S(1)} %copy-done.1, bf16[2048,896]{0,1:T(8,128)(2,1)S(1)} %copy-done), kind=kLoop, calls=%fused_computation | loop fusion | flops 58720256 | bytes 29360128 | tf_op jit(solution)/shard_map/concatenate | solution.py:90
  328.0 18.8 %copy.12 = bf16[2048,3584]{1,0:T(8,128)(2,1)} copy(bf16[2048,3584]{0,1:T(8,128)(2,1)} %pad_maximum_fusion) | data formatting | bytes 29360128
  346.8 3.8 convolution_convert_fusion.7
  350.7 3.3 convolution_convert_fusion.6
  354.0 3.3 convolution_convert_fusion.5
  357.3 3.3 convolution_convert_fusion.4
  360.6 31.3 %pad_maximum_fusion.1 = bf16[2048,3584]{0,1:T(8,128)(2,1)} fusion(bf16[2048,896]{0,1:T(8,128)(2,1)S(1)} %convolution_convert_fusion.4, bf16[2048,896]{0,1:T(8,128)(2,1)S(1)} %convolution_convert_fusion.5, bf16[2048,896]{0,1:T(8,128)(2,1)S(1)} %convolution_convert_fusion.6, bf16[2048,896]{0,1:T(8,128)(2,1)S(1)} %convolution_convert_fusion.7), kind=kLoop, calls=%fused_computation.1 | loop fusion | flops 58720256 | bytes 29360128 | tf_op jit(solution)/shard_map/concatenate | solution.py:91
  391.8 18.6 %copy.13 = bf16[2048,3584]{1,0:T(8,128)(2,1)} copy(bf16[2048,3584]{0,1:T(8,128)(2,1)} %pad_maximum_fusion.1) | data formatting | bytes 29360128
  410.5 3.8 convolution_convert_fusion.3
  424.2 31.1 %pad_maximum_fusion.2 = bf16[3584,2048]{1,0:T(8,128)(2,1)} fusion(bf16[896,2048]{1,0:T(8,128)(2,1)S(1)} %convolution_convert_fusion, bf16[896,2048]{1,0:T(8,128)(2,1)S(1)} %convolution_convert_fusion.1, bf16[896,2048]{1,0:T(8,128)(2,1)S(1)} %convolution_convert_fusion.2, bf16[896,2048]{1,0:T(8,128)(2,1)S(1)} %convolution_convert_fusion.3), kind=kLoop, calls=%fused_computation.2 | loop fusion | flops 58720256 | bytes 29360128 | tf_op jit(solution)/shard_map/concatenate | solution.py:92
  (131 shorter events, 66.5 us)
Async XLA Ops:
  8.0 156.3 %reduce-scatter.5.cloned.1.call-start = ((), (), s32[]{:S(2)}) async-start(), calls=%async_computation.3 | async-start | bytes 655360 | tf_op jit(solution)/shard_map/reduce_scatter | solution.py:77
  9.1 33.3 %collective-permute-start = (f32[32,1]{0,1:T(1,128)S(1)}, f32[32,1]{0,1:T(1,128)S(1)}, u32[]{:S(2)}, u32[]{:S(2)}) collective-permute-start(f32[32,1]{0,1:T(1,128)S(1)} %bitcast.46), channel_id=1, source_target_pairs={{0,16},{16,0},{1,17},{17,1},{2,18},{18,2},{3,19},{19,3},{4,20},{20... | collective-permute-start | bytes 392 | tf_op jit(solution)/shard_map/ppermute | solution.py:24
  28.1 10.8 %copy-start.4 = (bf16[128,2048]{1,0:T(8,128)(2,1)}, bf16[128,2048]{1,0:T(8,128)(2,1)S(1)}, u32[]{:S(2)}) copy-start(bf16[128,2048]{1,0:T(8,128)(2,1)S(1)} %all_gather.25) | copy-start | bytes 1572868
  38.9 33.8 %slice-start = ((s8[14680064]{0:T(1024)(128)(4,1)}), s8[2097152]{0:T(1024)(128)(4,1)S(1)}, s32[]{:S(2)}) async-start(s8[14680064]{0:T(1024)(128)(4,1)} %bitcast.44), calls=%async_computation.10 | async-start | bytes 4194304
  42.4 35.7 %copy-start.15 = (bf16[128,896]{1,0:T(8,128)(2,1)}, bf16[128,896]{1,0:T(8,128)(2,1)S(1)}, u32[]{:S(2)}) copy-start(bf16[128,896]{1,0:T(8,128)(2,1)S(1)} %fusion.90) | copy-start | bytes 688132
  59.0 18.3 %copy-start.5 = (bf16[128,2048]{1,0:T(8,128)(2,1)}, bf16[128,2048]{1,0:T(8,128)(2,1)S(1)}, u32[]{:S(2)}) copy-start(bf16[128,2048]{1,0:T(8,128)(2,1)S(1)} %all_gather.24) | copy-start | bytes 1572868
  59.0 13.0 %copy-start.3 = (bf16[2048,3584]{1,0:T(8,128)(2,1)S(1)}, bf16[2048,3584]{1,0:T(8,128)(2,1)}, u32[]{:S(2)}) copy-start(bf16[2048,3584]{1,0:T(8,128)(2,1)} %param.9) | copy-start | bytes 44040196
  59.0 13.7 %slice-start.1 = ((s8[14680064]{0:T(1024)(128)(4,1)}), s8[4194304]{0:T(1024)(128)(4,1)S(1)}, s32[]{:S(2)}) async-start(s8[14680064]{0:T(1024)(128)(4,1)} %bitcast.44), calls=%async_computation.11 | async-start | bytes 8388608
  62.1 10.7 %slice-start.2 = ((s8[14680064]{0:T(1024)(128)(4,1)}), s8[4194304]{0:T(1024)(128)(4,1)S(1)}, s32[]{:S(2)}) async-start(s8[14680064]{0:T(1024)(128)(4,1)} %bitcast.44), calls=%async_computation.12 | async-start | bytes 8388608
  68.9 3.9 slice-start.3
  74.5 18.4 %collective-permute-start.4 = (bf16[128,2688]{1,0:T(8,128)(2,1)S(1)}, bf16[128,2688]{1,0:T(8,128)(2,1)S(1)}, u32[]{:S(2)}, u32[]{:S(2)}) collective-permute-start(bf16[128,2688]{1,0:T(8,128)(2,1)S(1)} %pad_maximum_fusion.6), channel_id=1, source_target_pairs={{0,16},{16,0},{1,17},{17,1},{2,18},{18,2},{3,19},{19,3},{4,20},{20... | collective-permute-start | bytes 2064392 | tf_op jit(solution)/shard_map/ppermute | solution.py:24
  75.2 32.5 %collective-permute-start.3 = (bf16[128,2688]{1,0:T(8,128)(2,1)S(1)}, bf16[128,2688]{1,0:T(8,128)(2,1)S(1)}, u32[]{:S(2)}, u32[]{:S(2)}) collective-permute-start(bf16[128,2688]{1,0:T(8,128)(2,1)S(1)} %pad_maximum_fusion.5), channel_id=1, source_target_pairs={{0,16},{16,0},{1,17},{17,1},{2,18},{18,2},{3,19},{19,3},{4,20},{20... | collective-permute-start | bytes 2064392 | tf_op jit(solution)/shard_map/ppermute | solution.py:24
  76.8 45.5 %collective-permute-start.2 = (bf16[128,2688]{1,0:T(8,128)(2,1)S(1)}, bf16[128,2688]{1,0:T(8,128)(2,1)S(1)}, u32[]{:S(2)}, u32[]{:S(2)}) collective-permute-start(bf16[128,2688]{1,0:T(8,128)(2,1)S(1)} %pad_maximum_fusion.4), channel_id=1, source_target_pairs={{0,16},{16,0},{1,17},{17,1},{2,18},{18,2},{3,19},{19,3},{4,20},{20... | collective-permute-start | bytes 2064392 | tf_op jit(solution)/shard_map/ppermute | solution.py:24
  78.2 51.5 %collective-permute-start.1 = (bf16[128,2688]{1,0:T(8,128)(2,1)S(1)}, bf16[128,2688]{1,0:T(8,128)(2,1)S(1)}, u32[]{:S(2)}, u32[]{:S(2)}) collective-permute-start(bf16[128,2688]{1,0:T(8,128)(2,1)S(1)} %pad_maximum_fusion.3), channel_id=1, source_target_pairs={{0,16},{16,0},{1,17},{17,1},{2,18},{18,2},{3,19},{19,3},{4,20},{20... | collective-permute-start | bytes 2064392 | tf_op jit(solution)/shard_map/ppermute | solution.py:24
  122.5 7.2 %copy-start.16 = (bf16[128,896]{1,0:T(8,128)(2,1)S(1)}, bf16[128,896]{1,0:T(8,128)(2,1)}, u32[]{:S(2)}) copy-start(bf16[128,896]{1,0:T(8,128)(2,1)} %copy-done.15) | copy-start | bytes 688132
  123.4 17.0 %copy-start.12 = (bf16[128,896]{1,0:T(8,128)(2,1)}, bf16[128,896]{1,0:T(8,128)(2,1)S(1)}, u32[]{:S(2)}) copy-start(bf16[128,896]{1,0:T(8,128)(2,1)S(1)} %get-tuple-element.14) | copy-start | bytes 688132
  124.7 8.8 %copy-start.7 = (bf16[128,896]{1,0:T(8,128)(2,1)}, bf16[128,896]{1,0:T(8,128)(2,1)S(1)}, u32[]{:S(2)}) copy-start(bf16[128,896]{1,0:T(8,128)(2,1)S(1)} %get-tuple-element.21) | copy-start | bytes 688132
  142.5 55.5 %reduce-scatter.3.cloned.1.call-start = ((), (), s32[]{:S(2)}) async-start(), calls=%async_computation.2 | async-start | bytes 655360 | tf_op jit(solution)/shard_map/reduce_scatter | solution.py:75
  151.0 4.3 copy-start.10
  151.0 6.2 %copy-start.8 = (bf16[128,896]{1,0:T(8,128)(2,1)S(1)}, bf16[128,896]{1,0:T(8,128)(2,1)}, u32[]{:S(2)}) copy-start(bf16[128,896]{1,0:T(8,128)(2,1)} %copy-done.7) | copy-start | bytes 688132
  154.7 5.5 %copy-start.13 = (bf16[128,896]{1,0:T(8,128)(2,1)S(1)}, bf16[128,896]{1,0:T(8,128)(2,1)}, u32[]{:S(2)}) copy-start(bf16[128,896]{1,0:T(8,128)(2,1)} %copy-done.12) | copy-start | bytes 688132
  154.7 45.1 %all-gather.7.cloned.1.call-start = ((), (), s32[]{:S(2)}) async-start(), calls=%async_computation.4 | async-start | bytes 2621440 | tf_op jit(solution)/shard_map/all_gather | solution.py:37
  155.3 52.9 %all-gather.9.cloned.1.call-start = ((), (), s32[]{:S(2)}) async-start(), calls=%async_computation.5 | async-start | bytes 3440640 | tf_op jit(solution)/shard_map/all_gather | solution.py:68
  157.2 40.8 %copy-start.20 = (bf16[32,2048]{1,0:T(8,128)(2,1)S(1)}, bf16[32,2048]{1,0:T(8,128)(2,1)}, u32[]{:S(2)}) copy-start(bf16[32,2048]{1,0:T(8,128)(2,1)} %param.11) | copy-start | bytes 393220
  157.2 79.0 %all-gather.11.cloned.1.call-start = ((), (), s32[]{:S(2)}) async-start(), calls=%async_computation.6 | async-start | bytes 3440640 | tf_op jit(solution)/shard_map/all_gather | solution.py:68
  159.2 105.4 %all-gather.13.cloned.1.call-start = ((), (), s32[]{:S(2)}) async-start(), calls=%async_computation.7 | async-start | bytes 3440640 | tf_op jit(solution)/shard_map/all_gather | solution.py:68
  160.1 132.2 %all-gather.15.cloned.1.call-start = ((), (), s32[]{:S(2)}) async-start(), calls=%async_computation.8 | async-start | bytes 3440640 | tf_op jit(solution)/shard_map/all_gather | solution.py:68
  161.1 249.3 %all-gather.17.cloned.1.call-start = ((), (), s32[]{:S(2)}) async-start(), calls=%async_computation.9 | async-start | bytes 2621440 | tf_op jit(solution)/shard_map/all_gather | solution.py:36
  165.5 32.6 %collective-permute-start.5 = (f32[32,1]{0,1:T(1,128)S(1)}, f32[32,1]{0,1:T(1,128)S(1)}, u32[]{:S(2)}, u32[]{:S(2)}) collective-permute-start(f32[32,1]{0,1:T(1,128)S(1)} %bitcast.47), channel_id=1, source_target_pairs={{0,16},{16,0},{1,17},{17,1},{2,18},{18,2},{3,19},{19,3},{4,20},{20... | collective-permute-start | bytes 392 | tf_op jit(solution)/shard_map/ppermute | solution.py:24
  199.8 36.4 %copy-start.23 = (bf16[512,2048]{1,0:T(8,128)(2,1)S(1)}, bf16[512,2048]{1,0:T(8,128)(2,1)}, u32[]{:S(2)}) copy-start(bf16[512,2048]{1,0:T(8,128)(2,1)} %all-gather.7.cloned.1.call-done) | copy-start | bytes 6291460
  292.3 4.5 copy-start.2
  328.0 18.8 %copy-start.22 = (bf16[512,2688]{1,0:T(8,128)(2,1)S(1)}, bf16[512,2688]{1,0:T(8,128)(2,1)}, u32[]{:S(2)}) copy-start(bf16[512,2688]{1,0:T(8,128)(2,1)} %all-gather.9.cloned.1.call-done) | copy-start | bytes 8257540
  (12 other events, 35.9 us)
Sparse Core Ops, SparseCore 0:
  142.7 21.5 reduce-scatter.4
  166.6 19.9 reduce-scatter.2
Sparse Core Ops, SparseCore 1:
  156.7 22.8 all-gather.6
  181.6 26.5 all-gather.8
  210.2 26.0 all-gather.10
  238.4 26.1 all-gather.12
  266.2 26.1 all-gather.14
  293.9 22.4 all-gather.16

commit v2 on v1

--- a/solution.py
+++ b/solution.py
@@ -1,6 +1,10 @@
+import functools
+
 import jax
 import jax.numpy as jnp
 from jax import lax
+from jax.experimental import pallas as pl
+from jax.experimental.pallas import tpu as pltpu
 from jax.sharding import PartitionSpec as P
 
 EPS = 1e-05
@@ -95,6 +99,291 @@
     return body
 
 
+MESH = pl.DeviceIdType.MESH
+
+
+def exchange_kernel(n_col, chunks, size, width, tok_ref, gain_ref, cot_ref, wg_hbm, wu_hbm, wd_hbm,
+                    mixed_ref, gn_ref, inv_ref, nall, call, gg_all, gu_all, h_all,
+                    wg, wu, wd, mine, sq_out, sq_in, part, peer, trio, acc_m, acc_g,
+                    w_sem, sq_sem, ring_send, ring_recv, x_send, x_recv,
+                    y_send, y_recv, c_send, c_recv, f_send, f_recv, l_sem,
+                    ay_send, ay_recv, ac_send, ac_recv, af_send, af_recv, al_sem):
+    row, col, dep = lax.axis_index("row"), lax.axis_index("col"), lax.axis_index("depth")
+    x_peer = {"row": 1 - row}
+    y_dep = lax.rem(dep + 2, 4)
+    y_peer = {"depth": y_dep}
+    c_peer = {"depth": dep + 1 - 2 * lax.rem(dep, 2)}
+    block = tok_ref.shape[0]
+    has_left, has_right = col > 0, col < n_col - 1
+
+    def cols_of(c):
+        return pl.ds(pl.multiple_of(c * size, size), size)
+
+    def w_copies(c):
+        return (
+            pltpu.make_async_copy(wd_hbm.at[cols_of(c), :], wd.at[c], w_sem.at[c, 0]),
+            pltpu.make_async_copy(wg_hbm.at[:, cols_of(c)], wg.at[c], w_sem.at[c, 1]),
+            pltpu.make_async_copy(wu_hbm.at[:, cols_of(c)], wu.at[c], w_sem.at[c, 2]),
+        )
+
+    @pl.loop(0, chunks)
+    def _(c):
+        for copy in w_copies(c):
+            copy.start()
+
+    barrier = pltpu.get_barrier_semaphore()
+    for peer_id in (x_peer, y_peer, c_peer):
+        pl.semaphore_signal(barrier, inc=1, device_id=peer_id, device_id_type=MESH)
+
+    @pl.when(has_left)
+    def _():
+        pl.semaphore_signal(barrier, inc=1, device_id={"col": col - 1}, device_id_type=MESH)
+
+    @pl.when(has_right)
+    def _():
+        pl.semaphore_signal(barrier, inc=1, device_id={"col": col + 1}, device_id_type=MESH)
+
+    own_rows = pl.ds(pl.multiple_of(col * block, block), block)
+    mine[1, own_rows, :] = cot_ref[...]
+    inputs = tok_ref[...].astype(F32)
+    sq_out[...] = jnp.broadcast_to(jnp.sum(inputs * inputs, axis=1, keepdims=True), sq_out.shape)
+    pl.semaphore_wait(barrier, 3 + has_left.astype(jnp.int32) + has_right.astype(jnp.int32))
+    sq_copy = pltpu.make_async_remote_copy(sq_out, sq_in, sq_sem.at[0], sq_sem.at[1], device_id=x_peer, device_id_type=MESH)
+    sq_copy.start()
+
+    def hop(which, step, way):
+        origin = col - step if way == 0 else col + step
+        target = col + 1 if way == 0 else col - 1
+        rows = pl.ds(pl.multiple_of(origin * block, block), block)
+        return pltpu.make_async_remote_copy(
+            mine.at[which, rows, :], mine.at[which, rows, :],
+            ring_send.at[which, step, way], ring_recv.at[which, step, way],
+            device_id={"col": target}, device_id_type=MESH)
+
+    def sends(which, step, act):
+        @pl.when((col - step >= 0) & has_right)
+        def _():
+            act(hop(which, step, 0))
+
+        @pl.when((col + step < n_col) & has_left)
+        def _():
+            act(hop(which, step, 1))
+
+    def arrive(which, step):
+        @pl.when(col - 1 - step >= 0)
+        def _():
+            rows = pl.ds(pl.multiple_of((col - 1 - step) * block, block), block)
+            pltpu.make_async_remote_copy(
+                mine.at[which, rows, :], mine.at[which, rows, :],
+                ring_send.at[which, step, 0], ring_recv.at[which, step, 0],
+                device_id={"col": col - 1}, device_id_type=MESH).wait_recv()
+
+        @pl.when(col + 1 + step < n_col)
+        def _():
+            rows = pl.ds(pl.multiple_of((col + 1 + step) * block, block), block)
+            pltpu.make_async_remote_copy(
+                mine.at[which, rows, :], mine.at[which, rows, :],
+                ring_send.at[which, step, 1], ring_recv.at[which, step, 1],
+                device_id={"col": col + 1}, device_id_type=MESH).wait_recv()
+
+    sends(1, 0, lambda copy: copy.start())
+    sq_copy.wait()
+    inv = lax.rsqrt((sq_out[...] + sq_in[...]) / width + EPS)
+    inv_ref[...] = inv
+    mine[0, own_rows, :] = (inputs * inv[:, :1] * gain_ref[...]).astype(BF)
+    sends(0, 0, lambda copy: copy.start())
+    for step in range(n_col - 1):
+        for which in (1, 0):
+            arrive(which, step)
+            if step + 1 < n_col - 1:
+                sends(which, step + 1, lambda copy: copy.start())
+    for step in range(n_col - 1):
+        for which in (1, 0):
+            sends(which, step, lambda copy: copy.wait_send())
+
+    def remote(src, dst, a, b, to):
+        return pltpu.make_async_remote_copy(src, dst, a, b, device_id=to, device_id_type=MESH)
+
+    def act_copies(which):
+        out = (nall, call)[which]
+        return (
+            remote(mine.at[which], out.at[dep], ay_send.at[which], ay_recv.at[which], y_peer),
+            remote(mine.at[which], out.at[dep], ac_send.at[which], ac_recv.at[which], c_peer),
+            pltpu.make_async_copy(mine.at[which], out.at[dep], al_sem.at[which]),
+        )
+
+    def act_forward(which):
+        out = (nall, call)[which]
+        return remote(out.at[y_dep], out.at[y_dep], af_send.at[which], af_recv.at[which], c_peer)
+
+    for which in (1, 0):
+        for copy in act_copies(which):
+            copy.start()
+
+    def x_copy(c):
+        return remote(part.at[c], peer.at[c], x_send.at[c], x_recv.at[c], x_peer)
+
+    @pl.loop(0, chunks)
+    def _(c):
+        for copy in w_copies(c):
+            copy.wait()
+        part[c, 2] = contract_cols(mine[1], wd[c]).astype(BF)
+        part[c, 0] = jnp.dot(mine[0], wg[c], preferred_element_type=F32).astype(BF)
+        part[c, 1] = jnp.dot(mine[0], wu[c], preferred_element_type=F32).astype(BF)
+        x_copy(c).start()
+
+    outs = (gg_all, gu_all, h_all)
+
+    def spread(c, k):
+        dst = outs[k].at[dep, :, cols_of(c)]
+        return (
+            remote(trio.at[c, k], dst, y_send.at[c, k], y_recv.at[c, k], y_peer),
+            remote(trio.at[c, k], dst, c_send.at[c, k], c_recv.at[c, k], c_peer),
+            pltpu.make_async_copy(trio.at[c, k], dst, l_sem.at[c, k]),
+        )
+
+    def forward(c, k):
+        ref = outs[k].at[y_dep, :, cols_of(c)]
+        return remote(ref, ref, f_send.at[c, k], f_recv.at[c, k], c_peer)
+
+    def pass_on(c):
+        for k in range(3):
+            spread(c, k)[0].wait_recv()
+            forward(c, k).start()
+
+    acc_m[...] = jnp.zeros_like(acc_m)
+    acc_g[...] = jnp.zeros_like(acc_g)
+    for which in (1, 0):
+        act_copies(which)[0].wait_recv()
+        act_forward(which).start()
+
+    @pl.loop(0, chunks)
+    def _(c):
+        x_copy(c).wait()
+        gate = part[c, 0].astype(F32) + peer[c, 0].astype(F32)
+        up = part[c, 1].astype(F32) + peer[c, 1].astype(F32)
+        grad_hidden = part[c, 2].astype(F32) + peer[c, 2].astype(F32)
+        sig = jax.nn.sigmoid(gate)
+        act = gate * sig
+        trio[c, 2] = (act * up).astype(BF)
+        trio[c, 1] = (grad_hidden * act).astype(BF)
+        trio[c, 0] = (grad_hidden * up * sig * (1.0 + gate * (1.0 - sig))).astype(BF)
+        for k in range(3):
+            for copy in spread(c, k):
+                copy.start()
+        acc_m[...] += jnp.dot(trio[c, 2], wd[c], preferred_element_type=F32)
+        acc_g[...] += contract_cols(trio[c, 0], wg[c]) + contract_cols(trio[c, 1], wu[c])
+
+        @pl.when(c > 0)
+        def _():
+            pass_on(c - 1)
+
+    mixed_ref[...] = acc_m[...].astype(BF)
+    gn_ref[...] = acc_g[...].astype(BF)
+    pass_on(chunks - 1)
+    for which in (1, 0):
+        y_one, c_one, l_one = act_copies(which)
+        y_one.wait_send()
+        c_one.wait()
+        l_one.wait()
+        act_forward(which).wait()
+
+    @pl.loop(0, chunks)
+    def _(c):
+        for k in range(3):
+            y_one, c_one, l_one = spread(c, k)
+            y_one.wait_send()
+            c_one.wait()
+            l_one.wait()
+            forward(c, k).wait()
+
+
+def exchange(mesh, tokens, norm_gain, cotangent, w_gate, w_up, w_down):
+    n_col = mesh.shape["col"]
+    block, feat = tokens.shape
+    hidden = w_gate.shape[1]
+    size = next(s for s in (512, 256, 128) if hidden % s == 0)
+    chunks = hidden // size
+    rows = block * n_col
+    sds = jax.ShapeDtypeStruct
+    dma = pltpu.SemaphoreType.DMA
+    vmem, hbm = pl.BlockSpec(memory_space=pltpu.VMEM), pl.BlockSpec(memory_space=pl.ANY)
+    return pl.pallas_call(
+        functools.partial(exchange_kernel, n_col, chunks, size, feat * 2),
+        out_shape=[sds((rows, feat), BF)] * 2 + [sds((block, 128), F32)]
+        + [sds((4, rows, feat), BF)] * 2 + [sds((4, rows, hidden), BF)] * 3,
+        in_specs=[vmem] * 3 + [hbm] * 3,
+        out_specs=[vmem] * 3 + [hbm] * 5,
+        scratch_shapes=[
+            pltpu.VMEM((chunks, feat, size), BF),
+            pltpu.VMEM((chunks, feat, size), BF),
+            pltpu.VMEM((chunks, size, feat), BF),
+            pltpu.VMEM((2, rows, feat), BF),
+            pltpu.VMEM((block, 128), F32),
+            pltpu.VMEM((block, 128), F32),
+            pltpu.VMEM((chunks, 3, rows, size), BF),
+            pltpu.VMEM((chunks, 3, rows, size), BF),
+            pltpu.VMEM((chunks, 3, rows, size), BF),
+            pltpu.VMEM((rows, feat), F32),
+            pltpu.VMEM((rows, feat), F32),
+            dma((chunks, 3)), dma((2,)), dma((2, n_col, 2)), dma((2, n_col, 2)), dma((chunks,)), dma((chunks,)),
+        ] + [dma((chunks, 3))] * 7 + [dma((2,))] * 7,
+        compiler_params=pltpu.CompilerParams(
+            collective_id=0, has_side_effects=True, vmem_limit_bytes=62 * 1024 * 1024
+        ),
+        cost_estimate=pl.CostEstimate(
+            flops=12 * rows * feat * hidden, bytes_accessed=6 * feat * hidden + 24 * rows * hidden,
+            transcendentals=rows * hidden),
+    )(tokens, norm_gain[None, :], cotangent, w_gate, w_up, w_down)
+
+
+def make_fused(mesh):
+    n_col = mesh.shape["col"]
+
+    def swap_add(value, axis, bit):
+        count = mesh.shape[axis]
+        return value + lax.ppermute(value, axis, [(i, i ^ bit) for i in range(count)])
+
+    def body(tokens, norm_gain, w_gate, w_up, w_down, cotangent):
+        width = tokens.shape[1] * 2
+        mixed, grad_normed, inv, nall, call, gg_all, gu_all, h_all = exchange(
+            mesh, tokens, norm_gain, cotangent, w_gate, w_up, w_down)
+        mixed, grad_normed = (
+            lax.psum_scatter(value, "col", scatter_dimension=0, tiled=True).astype(F32)
+            for value in (mixed, grad_normed)
+        )
+        nall, call, gg_all, gu_all, h_all = (
+            value.reshape(-1, value.shape[2]) for value in (nall, call, gg_all, gu_all, h_all))
+        grad_gate = contract_rows(nall, gg_all).astype(BF)
+        grad_up = contract_rows(nall, gu_all).astype(BF)
+        grad_down = contract_rows(h_all, call).astype(BF)
+        inputs = tokens.astype(F32)
+        inv_rms = inv[:, :1]
+        normal_rows = inputs * inv_rms
+        output = (inputs + mixed).astype(BF)
+        grad_scaled = grad_normed * norm_gain[None, :]
+        proj = swap_add(jnp.sum(grad_scaled * normal_rows, axis=1, keepdims=True), "row", 1)
+        grad_tokens = (
+            cotangent.astype(F32) + inv_rms * (grad_scaled - normal_rows * (proj / width))
+        ).astype(BF)
+        grad_gain = jnp.sum(grad_normed * normal_rows, axis=0)
+        for axis in ("depth", "col"):
+            bit = 1
+            while bit < mesh.shape[axis]:
+                grad_gain = swap_add(grad_gain, axis, bit)
+                bit *= 2
+        return output, grad_tokens, grad_gain, grad_gate, grad_up, grad_down
+
+    return body
+
+
+def pick_body(mesh):
+    shape = mesh.shape
+    if shape["row"] == 2 and shape["depth"] == 4 and shape["col"] == 4:
+        return make_fused(mesh)
+    return make_body(mesh)
+
+
 def solution(mesh):
     in_specs = (
         P(("col", "depth"), "row"),
@@ -113,5 +402,5 @@
         P("col", "row"),
     )
     return jax.shard_map(
-        make_body(mesh), mesh=mesh, in_specs=in_specs, out_specs=out_specs, check_vma=False
+        pick_body(mesh), mesh=mesh, in_specs=in_specs, out_specs=out_specs, check_vma=False
     )

time: 468 us -> 184 us (0.39); the launches traced: 463 us -> 184 us
  waiting for transfers between devices: 127 us -> 13.7 us
  Pallas kernels: 0 us -> 110 us
  other arithmetic: 107 us -> 3.46 us
  blocking collectives: 63.6 us -> 0 us
  matrix products: 101 us -> 37.9 us
  local copies, waits for them, and re-layouts: 38.7 us -> 0.85 us
  starting transfers between devices: 9.11 us -> 3.95 us
    pallas_call x0 -> x1, Pallas kernels: none -> 110 us  [exchange(): pl.pallas_call(functools.partial(exchange_kernel, n_col, chunks, size, fe...]
    concatenate x11 -> x0, other arithmetic: 99.2 us -> none  [the longest x1 31.3 us: body(): jnp.concatenate(ups, axis=1)]
    all_gather x6 -> x0, waiting for transfers between devices: 76.5 us -> none  [the longest x4 76.5 us: body(): trios.append(lax.all_gather(trio, 'depth', axis=0, tiled=True))]
    dot_general x24 -> x0, matrix products: 53.7 us -> none  [the longest x12 25.9 us: contract_cols(): lax.dot_general(left, right, (((1,), (1,)), ((), ())), preferred_element_...]
    ppermute x6 -> x5, waiting for transfers between devices: 47.3 us -> 5.75 us  [swap_add(): lax.ppermute(value, axis, [(i, i ^ bit) for i in range(count)])]
    unnamed x62 -> x12, local copies, waits for them, and re-layouts: 38.7 us -> 0.03 us
    all_gather x2 -> x0, blocking collectives: 32.4 us -> none  [the longest x1 16.5 us: body(): normed_mine = lax.all_gather(normed, 'col', axis=0, tiled=True)]
    psum x1 -> x0, blocking collectives: 31.1 us -> none  [body(): lax.psum(jnp.sum(grad_normed * normal_rows, axis=0), ('col', 'depth'))]
  transfers between devices with their start and end apart: 14 -> 7, of which waited for: 9 -> 4; matrix products, arithmetic and copies ran while one was open for 37% -> 23% of each run, Pallas kernels for 0% -> 0%
where the time goes in v2:
time: 184 us
  Pallas kernels  110 us (60%)
  matrix products  37.9 us (21%)
  between operations  14.1 us (8%)
  waiting for transfers between devices  13.7 us (7%)
  starting transfers between devices  3.95 us (2%)
  other arithmetic  3.46 us (2%)
    pallas_call x1, Pallas kernels, exchange(): pl.pallas_call(functools.partial(exchange_kernel, n_col, chunks, size, fe...  110 us
    dot_general x3, matrix products, contract_rows(): lax.dot_general(left, right, (((0,), (0,)), ((), ())), preferred_element_...  37.9 us
    reduce_scatter x2, waiting for transfers between devices, body(): lax.psum_scatter(value, 'col', scatter_dimension=0, tiled=True).astype(F32)  7.41 us
    ppermute x5, waiting for transfers between devices, swap_add(): lax.ppermute(value, axis, [(i, i ^ bit) for i in range(count)])  5.75 us
    ppermute x5, starting transfers between devices, swap_add(): lax.ppermute(value, axis, [(i, i ^ bit) for i in range(count)])  3.69 us
  transfers between devices with their start and end apart: 7, of which 4 were waited for; matrix products, arithmetic and copies ran while one was open for 23% of the time, Pallas kernels for 0%

profile of v2, /device:TPU:0, one launch (start us, length us, event | category | flops | bytes accessed | tf_op | source)
XLA Modules:
  0.0 183.8 jit_solution(4290596483726825668)
XLA Ops:
  7.2 0.0 reduce-scatter.5.cloned.1.call-start
  7.2 109.8 %shard_map.109 = (bf16[128,2048]{1,0:T(8,128)(2,1)}, bf16[128,2048]{1,0:T(8,128)(2,1)}, f32[32,128]{1,0:T(8,128)}, bf16[4,128,2048]{2,1,0:T(8,128)(2,1)}, bf16[4...) custom-call(bf16[32,2048]{1,0:T(8,128)(2,1)} %tok_ref.1, ...), custom_call_target="tpu_custom_call" | custom-call | flops 11274289152 | bytes 55050240 | tf_op jit(solution)/shard_map/pallas_call | solution.py:311
  117.0 0.0 reduce-scatter.5.cloned.1.call-update
  117.1 0.2 reduce-scatter.3.cloned.1.call-start
  117.3 0.5 reduce-scatter.3.cloned.1.call-update
  117.8 0.8 slice_reduce_fusion
  118.7 0.0 copy-start.3
  118.7 0.0 copy-start.5
  118.7 13.4 %bitcast_convert_fusion = bf16[3584,2048]{1,0:T(8,128)(2,1)} fusion(bf16[4,128,3584]{2,1,0:T(8,128)(2,1)} %get-tuple-element.20, bf16[4,128,2048]{2,1,0:T(8,128)(2,1)} %get-tuple-element.21), kind=kOutput, calls=%fused_computation | convolution fusion | flops 7523532800 | bytes 20447232 | tf_op jit(solution)/shard_map/dot_general | solution.py:16
  132.1 7.4 %reduce-scatter.5.cloned.1.call-done = bf16[32,2048]{1,0:T(8,128)(2,1)} async-done(((bf16[128,2048]{1,0:T(8,128)(2,1)}), bf16[32,2048]{1,0:T(8,128)(2,1)}) %reduce-scatter.5.cloned.1.call-update) | async-done | bytes 131088 | tf_op jit(solution)/shard_map/reduce_scatter | solution.py:352
  139.5 0.0 copy-done
  139.5 0.0 copy-done.3
  139.5 1.2 fusion.8
  140.6 0.1 collective-permute-start.1
  140.7 0.0 copy-done.5
  140.7 0.0 copy-start.4
  140.7 13.4 %bitcast_convert_fusion.2 = bf16[2048,3584]{1,0:T(8,128)(2,1)} fusion(bf16[4,128,2048]{2,1,0:T(8,128)(2,1)S(1)} %copy-done.5, bf16[4,128,3584]{2,1,0:T(8,128)(2,1)} %get-tuple-element.18), kind=kOutput, calls=%fused_computation.2 | convolution fusion | flops 7523532800 | bytes 20447232 | tf_op jit(solution)/shard_map/dot_general | solution.py:16
  154.1 0.0 collective-permute-done.1
  154.1 1.4 collective-permute-start.2
  155.5 0.0 copy-done.4
  155.5 11.2 %bitcast_convert_fusion.1 = bf16[2048,3584]{1,0:T(8,128)(2,1)} fusion(bf16[4,128,2048]{2,1,0:T(8,128)(2,1)S(1)} %copy-done.5, bf16[4,128,3584]{2,1,0:T(8,128)(2,1)S(1)} %copy-done.4), kind=kOutput, calls=%fused_computation.1 | convolution fusion | flops 7523532800 | bytes 20447232 | tf_op jit(solution)/shard_map/dot_general | solution.py:16
  166.7 1.4 collective-permute-start
  168.2 0.0 collective-permute-done.2
  168.2 0.0 collective-permute-start.3
  168.2 2.1 %collective-permute-done = f32[32,1]{0,1:T(1,128)S(1)} collective-permute-done((f32[32,1]{0,1:T(1,128)S(1)}, f32[32,1]{0,1:T(1,128)S(1)}, u32[]{:S(2)}, u32[]{:S(2)}) %collective-permute-start) | collective-permute-done | bytes 160 | tf_op jit(solution)/shard_map/ppermute | solution.py:345
  170.3 1.6 collective-permute-done.3
  171.8 0.7 collective-permute-start.4
  172.6 0.0 copy-done.1
  172.6 0.0 copy-done.2
  172.6 1.7 fusion.5
  174.3 2.1 %collective-permute-done.4 = f32[2048]{0:T(1024)S(1)} collective-permute-done((f32[2048]{0:T(1024)S(1)}, f32[2048]{0:T(1024)S(1)}, u32[]{:S(2)}, u32[]{:S(2)}) %collective-permute-start.4) | collective-permute-done | bytes 8224 | tf_op jit(solution)/shard_map/ppermute | solution.py:345
  176.4 0.6 add.31
  (8 shorter events, 0.0 us)
Async XLA Ops:
  7.2 132.3 %reduce-scatter.5.cloned.1.call-start = ((), (), s32[]{:S(2)}) async-start(), calls=%async_computation.3 | async-start | bytes 655360 | tf_op jit(solution)/shard_map/reduce_scatter | solution.py:352
  117.1 55.5 %reduce-scatter.3.cloned.1.call-start = ((), (), s32[]{:S(2)}) async-start(), calls=%async_computation.2 | async-start | bytes 655360 | tf_op jit(solution)/shard_map/reduce_scatter | solution.py:352
  118.6 20.8 %copy-start = (bf16[32,2048]{1,0:T(8,128)(2,1)S(1)}, bf16[32,2048]{1,0:T(8,128)(2,1)}, u32[]{:S(2)}) copy-start(bf16[32,2048]{1,0:T(8,128)(2,1)} %tok_ref.1) | copy-start | bytes 393220
  118.7 20.8 %copy-start.3 = (f32[2048]{0:T(1024)S(1)}, f32[2048]{0:T(1024)}, u32[]{:S(2)}) copy-start(f32[2048]{0:T(1024)} %param.7) | copy-start | bytes 24580
  118.7 22.1 %copy-start.5 = (bf16[4,128,2048]{2,1,0:T(8,128)(2,1)S(1)}, bf16[4,128,2048]{2,1,0:T(8,128)(2,1)}, u32[]{:S(2)}) copy-start(bf16[4,128,2048]{2,1,0:T(8,128)(2,1)} %get-tuple-element.17) | copy-start | bytes 6291460
  140.6 13.5 %collective-permute-start.1 = (f32[2048]{0:T(1024)S(1)}, f32[2048]{0:T(1024)S(1)}, u32[]{:S(2)}, u32[]{:S(2)}) collective-permute-start(f32[2048]{0:T(1024)S(1)} %get-tuple-element.22), channel_id=1, source_target_pairs={{0,1},{1,0},{2,3},{3,2},{4,5},{5,4},{6,7},{7,6},{8,9},{9,8},{10,11... | collective-permute-start | bytes 24584 | tf_op jit(solution)/shard_map/ppermute | solution.py:345
  140.7 14.8 %copy-start.4 = (bf16[4,128,3584]{2,1,0:T(8,128)(2,1)S(1)}, bf16[4,128,3584]{2,1,0:T(8,128)(2,1)}, u32[]{:S(2)}) copy-start(bf16[4,128,3584]{2,1,0:T(8,128)(2,1)} %get-tuple-element.19) | copy-start | bytes 11010052
  154.1 14.1 %collective-permute-start.2 = (f32[2048]{0:T(1024)S(1)}, f32[2048]{0:T(1024)S(1)}, u32[]{:S(2)}, u32[]{:S(2)}) collective-permute-start(f32[2048]{0:T(1024)S(1)} %add.28), channel_id=1, source_target_pairs={{0,2},{1,3},{2,0},{3,1},{4,6},{5,7},{6,4},{7,5},{8,10},{9,11},{10,... | collective-permute-start | bytes 24584 | tf_op jit(solution)/shard_map/ppermute | solution.py:345
  155.5 17.0 %copy-start.1 = (bf16[32,2048]{1,0:T(8,128)(2,1)S(1)}, bf16[32,2048]{1,0:T(8,128)(2,1)}, u32[]{:S(2)}) copy-start(bf16[32,2048]{1,0:T(8,128)(2,1)} %cot_ref.1) | copy-start | bytes 393220
  155.5 17.0 %copy-start.2 = (bf16[32,2048]{1,0:T(8,128)(2,1)S(1)}, bf16[32,2048]{1,0:T(8,128)(2,1)}, u32[]{:S(2)}) copy-start(bf16[32,2048]{1,0:T(8,128)(2,1)} %reduce-scatter.5.cloned.1.call-done) | copy-start | bytes 393220
  166.7 3.5 %collective-permute-start = (f32[32,1]{0,1:T(1,128)S(1)}, f32[32,1]{0,1:T(1,128)S(1)}, u32[]{:S(2)}, u32[]{:S(2)}) collective-permute-start(f32[32,1]{0,1:T(1,128)S(1)} %bitcast.18), channel_id=1, source_target_pairs={{0,16},{16,0},{1,17},{17,1},{2,18},{18,2},{3,19},{19,3},{4,20},{20... | collective-permute-start | bytes 392 | tf_op jit(solution)/shard_map/ppermute | solution.py:345
  168.2 3.7 %collective-permute-start.3 = (f32[2048]{0:T(1024)S(1)}, f32[2048]{0:T(1024)S(1)}, u32[]{:S(2)}, u32[]{:S(2)}) collective-permute-start(f32[2048]{0:T(1024)S(1)} %add.29), channel_id=1, source_target_pairs={{0,4},{4,0},{8,12},{12,8},{1,5},{5,1},{9,13},{13,9},{2,6},{6,2},{1... | collective-permute-start | bytes 24584 | tf_op jit(solution)/shard_map/ppermute | solution.py:345
  171.8 4.5 %collective-permute-start.4 = (f32[2048]{0:T(1024)S(1)}, f32[2048]{0:T(1024)S(1)}, u32[]{:S(2)}, u32[]{:S(2)}) collective-permute-start(f32[2048]{0:T(1024)S(1)} %add.30), channel_id=1, source_target_pairs={{0,8},{4,12},{8,0},{12,4},{1,9},{5,13},{9,1},{13,5},{2,10},{6,14},... | collective-permute-start | bytes 24584 | tf_op jit(solution)/shard_map/ppermute | solution.py:345
Sparse Core Ops, SparseCore 0:
  117.2 22.2 reduce-scatter.4
  141.8 19.9 reduce-scatter.2

commit v3 on v2

--- a/solution.py
+++ b/solution.py
@@ -104,20 +104,22 @@
 
 def exchange_kernel(n_col, chunks, size, width, tok_ref, gain_ref, cot_ref, wg_hbm, wu_hbm, wd_hbm,
                     mixed_ref, gn_ref, inv_ref, nall, call, gg_all, gu_all, h_all,
-                    wg, wu, wd, mine, sq_out, sq_in, part, peer, trio, acc_m, acc_g,
+                    wg, wu, wd, both, sq_out, sq_in, part, peer, trio, acc_m, acc_g, end_out, end_in,
                     w_sem, sq_sem, ring_send, ring_recv, x_send, x_recv,
                     y_send, y_recv, c_send, c_recv, f_send, f_recv, l_sem,
-                    ay_send, ay_recv, ac_send, ac_recv, af_send, af_recv, al_sem):
+                    ay_send, ay_recv, ac_send, ac_recv, af_send, af_recv, al_sem, e_send, e_recv):
     row, col, dep = lax.axis_index("row"), lax.axis_index("col"), lax.axis_index("depth")
     x_peer = {"row": 1 - row}
-    y_dep = lax.rem(dep + 2, 4)
-    y_peer = {"depth": y_dep}
-    c_peer = {"depth": dep + 1 - 2 * lax.rem(dep, 2)}
+    me = lax.rem(dep, 2)
+    y_peer = {"depth": lax.rem(dep + 2, 4)}
+    c_peer = {"depth": dep + 1 - 2 * me}
+    chip = pl.ds(dep - me, 2)
+    y_chip = pl.ds(lax.rem(dep - me + 2, 4), 2)
     block = tok_ref.shape[0]
     has_left, has_right = col > 0, col < n_col - 1
 
     def cols_of(c):
-        return pl.ds(pl.multiple_of(c * size, size), size)
+        return pl.ds(pl.multiple_of((me * chunks + c) * size, size), size)
 
     def w_copies(c):
         return (
@@ -144,7 +146,7 @@
         pl.semaphore_signal(barrier, inc=1, device_id={"col": col + 1}, device_id_type=MESH)
 
     own_rows = pl.ds(pl.multiple_of(col * block, block), block)
-    mine[1, own_rows, :] = cot_ref[...]
+    both[1, me, own_rows, :] = cot_ref[...]
     inputs = tok_ref[...].astype(F32)
     sq_out[...] = jnp.broadcast_to(jnp.sum(inputs * inputs, axis=1, keepdims=True), sq_out.shape)
     pl.semaphore_wait(barrier, 3 + has_left.astype(jnp.int32) + has_right.astype(jnp.int32))
@@ -156,7 +158,7 @@
         target = col + 1 if way == 0 else col - 1
         rows = pl.ds(pl.multiple_of(origin * block, block), block)
         return pltpu.make_async_remote_copy(
-            mine.at[which, rows, :], mine.at[which, rows, :],
+            both.at[which, me, rows, :], both.at[which, me, rows, :],
             ring_send.at[which, step, way], ring_recv.at[which, step, way],
             device_id={"col": target}, device_id_type=MESH)
 
@@ -174,7 +176,7 @@
         def _():
             rows = pl.ds(pl.multiple_of((col - 1 - step) * block, block), block)
             pltpu.make_async_remote_copy(
-                mine.at[which, rows, :], mine.at[which, rows, :],
+                both.at[which, me, rows, :], both.at[which, me, rows, :],
                 ring_send.at[which, step, 0], ring_recv.at[which, step, 0],
                 device_id={"col": col - 1}, device_id_type=MESH).wait_recv()
 
@@ -182,7 +184,7 @@
         def _():
             rows = pl.ds(pl.multiple_of((col + 1 + step) * block, block), block)
             pltpu.make_async_remote_copy(
-                mine.at[which, rows, :], mine.at[which, rows, :],
+                both.at[which, me, rows, :], both.at[which, me, rows, :],
                 ring_send.at[which, step, 1], ring_recv.at[which, step, 1],
                 device_id={"col": col + 1}, device_id_type=MESH).wait_recv()
 
@@ -190,7 +192,7 @@
     sq_copy.wait()
     inv = lax.rsqrt((sq_out[...] + sq_in[...]) / width + EPS)
     inv_ref[...] = inv
-    mine[0, own_rows, :] = (inputs * inv[:, :1] * gain_ref[...]).astype(BF)
+    both[0, me, own_rows, :] = (inputs * inv[:, :1] * gain_ref[...]).astype(BF)
     sends(0, 0, lambda copy: copy.start())
     for step in range(n_col - 1):
         for which in (1, 0):
@@ -204,21 +206,26 @@
     def remote(src, dst, a, b, to):
         return pltpu.make_async_remote_copy(src, dst, a, b, device_id=to, device_id_type=MESH)
 
-    def act_copies(which):
+    def y_act(which):
         out = (nall, call)[which]
-        return (
-            remote(mine.at[which], out.at[dep], ay_send.at[which], ay_recv.at[which], y_peer),
-            remote(mine.at[which], out.at[dep], ac_send.at[which], ac_recv.at[which], c_peer),
-            pltpu.make_async_copy(mine.at[which], out.at[dep], al_sem.at[which]),
-        )
+        return remote(both.at[which, me], out.at[dep], ay_send.at[which], ay_recv.at[which], y_peer)
+
+    def c_act(which):
+        return remote(both.at[which, me], both.at[which, me], ac_send.at[which], ac_recv.at[which], c_peer)
+
+    def own_act(which):
+        return pltpu.make_async_copy(both.at[which], (nall, call)[which].at[chip], al_sem.at[which])
 
     def act_forward(which):
-        out = (nall, call)[which]
-        return remote(out.at[y_dep], out.at[y_dep], af_send.at[which], af_recv.at[which], c_peer)
+        ref = (nall, call)[which].at[lax.rem(dep + 2, 4)]
+        return remote(ref, ref, af_send.at[which], af_recv.at[which], c_peer)
 
     for which in (1, 0):
-        for copy in act_copies(which):
-            copy.start()
+        c_act(which).start()
+        y_act(which).start()
+    for which in (1, 0):
+        c_act(which).wait()
+        own_act(which).start()
 
     def x_copy(c):
         return remote(part.at[c], peer.at[c], x_send.at[c], x_recv.at[c], x_peer)
@@ -227,15 +234,18 @@
     def _(c):
         for copy in w_copies(c):
             copy.wait()
-        part[c, 2] = contract_cols(mine[1], wd[c]).astype(BF)
-        part[c, 0] = jnp.dot(mine[0], wg[c], preferred_element_type=F32).astype(BF)
-        part[c, 1] = jnp.dot(mine[0], wu[c], preferred_element_type=F32).astype(BF)
+        cot_rows = both[1].reshape(-1, both.shape[3])
+        norm_rows = both[0].reshape(-1, both.shape[3])
+        shape = part.shape[2:]
+        part[c, 2] = contract_cols(cot_rows, wd[c]).astype(BF).reshape(shape)
+        part[c, 0] = jnp.dot(norm_rows, wg[c], preferred_element_type=F32).astype(BF).reshape(shape)
+        part[c, 1] = jnp.dot(norm_rows, wu[c], preferred_element_type=F32).astype(BF).reshape(shape)
         x_copy(c).start()
 
     outs = (gg_all, gu_all, h_all)
 
     def spread(c, k):
-        dst = outs[k].at[dep, :, cols_of(c)]
+        dst = outs[k].at[chip, :, cols_of(c)]
         return (
             remote(trio.at[c, k], dst, y_send.at[c, k], y_recv.at[c, k], y_peer),
             remote(trio.at[c, k], dst, c_send.at[c, k], c_recv.at[c, k], c_peer),
@@ -243,7 +253,7 @@
         )
 
     def forward(c, k):
-        ref = outs[k].at[y_dep, :, cols_of(c)]
+        ref = outs[k].at[y_chip, :, cols_of(c)]
         return remote(ref, ref, f_send.at[c, k], f_recv.at[c, k], c_peer)
 
     def pass_on(c):
@@ -254,7 +264,7 @@
     acc_m[...] = jnp.zeros_like(acc_m)
     acc_g[...] = jnp.zeros_like(acc_g)
     for which in (1, 0):
-        act_copies(which)[0].wait_recv()
+        y_act(which).wait_recv()
         act_forward(which).start()
 
     @pl.loop(0, chunks)
@@ -271,22 +281,31 @@
         for k in range(3):
             for copy in spread(c, k):
                 copy.start()
-        acc_m[...] += jnp.dot(trio[c, 2], wd[c], preferred_element_type=F32)
-        acc_g[...] += contract_cols(trio[c, 0], wg[c]) + contract_cols(trio[c, 1], wu[c])
+        flat = [trio[c, k].reshape(-1, size) for k in range(3)]
+        shape = acc_m.shape
+        acc_m[...] += jnp.dot(flat[2], wd[c], preferred_element_type=F32).reshape(shape)
+        acc_g[...] += (contract_cols(flat[0], wg[c]) + contract_cols(flat[1], wu[c])).reshape(shape)
 
         @pl.when(c > 0)
         def _():
             pass_on(c - 1)
 
-    mixed_ref[...] = acc_m[...].astype(BF)
-    gn_ref[...] = acc_g[...].astype(BF)
+    def end_copy(k):
+        return remote(end_out.at[k], end_in.at[k], e_send.at[k], e_recv.at[k], c_peer)
+
+    end_out[0] = acc_m[1 - me].astype(BF)
+    end_copy(0).start()
+    end_out[1] = acc_g[1 - me].astype(BF)
+    end_copy(1).start()
     pass_on(chunks - 1)
     for which in (1, 0):
-        y_one, c_one, l_one = act_copies(which)
-        y_one.wait_send()
-        c_one.wait()
-        l_one.wait()
+        y_act(which).wait_send()
+        own_act(which).wait()
         act_forward(which).wait()
+    end_copy(0).wait()
+    mixed_ref[...] = (acc_m[me] + end_in[0].astype(F32)).astype(BF)
+    end_copy(1).wait()
+    gn_ref[...] = (acc_g[me] + end_in[1].astype(F32)).astype(BF)
 
     @pl.loop(0, chunks)
     def _(c):
@@ -302,8 +321,8 @@
     n_col = mesh.shape["col"]
     block, feat = tokens.shape
     hidden = w_gate.shape[1]
-    size = next(s for s in (512, 256, 128) if hidden % s == 0)
-    chunks = hidden // size
+    size = next(s for s in (256, 128) if hidden % (2 * s) == 0)
+    chunks = hidden // (2 * size)
     rows = block * n_col
     sds = jax.ShapeDtypeStruct
     dma = pltpu.SemaphoreType.DMA
@@ -318,16 +337,18 @@
             pltpu.VMEM((chunks, feat, size), BF),
             pltpu.VMEM((chunks, feat, size), BF),
             pltpu.VMEM((chunks, size, feat), BF),
-            pltpu.VMEM((2, rows, feat), BF),
+            pltpu.VMEM((2, 2, rows, feat), BF),
             pltpu.VMEM((block, 128), F32),
             pltpu.VMEM((block, 128), F32),
-            pltpu.VMEM((chunks, 3, rows, size), BF),
-            pltpu.VMEM((chunks, 3, rows, size), BF),
-            pltpu.VMEM((chunks, 3, rows, size), BF),
-            pltpu.VMEM((rows, feat), F32),
-            pltpu.VMEM((rows, feat), F32),
+            pltpu.VMEM((chunks, 3, 2, rows, size), BF),
+            pltpu.VMEM((chunks, 3, 2, rows, size), BF),
+            pltpu.VMEM((chunks, 3, 2, rows, size), BF),
+            pltpu.VMEM((2, rows, feat), F32),
+            pltpu.VMEM((2, rows, feat), F32),
+            pltpu.VMEM((2, rows, feat), BF),
+            pltpu.VMEM((2, rows, feat), BF),
             dma((chunks, 3)), dma((2,)), dma((2, n_col, 2)), dma((2, n_col, 2)), dma((chunks,)), dma((chunks,)),
-        ] + [dma((chunks, 3))] * 7 + [dma((2,))] * 7,
+        ] + [dma((chunks, 3))] * 7 + [dma((2,))] * 9,
         compiler_params=pltpu.CompilerParams(
             collective_id=0, has_side_effects=True, vmem_limit_bytes=62 * 1024 * 1024
         ),
@@ -356,6 +377,8 @@
             value.reshape(-1, value.shape[2]) for value in (nall, call, gg_all, gu_all, h_all))
         grad_gate = contract_rows(nall, gg_all).astype(BF)
         grad_up = contract_rows(nall, gu_all).astype(BF)
+        mixed, grad_normed, grad_gate, grad_up, h_all, call = lax.optimization_barrier(
+            (mixed, grad_normed, grad_gate, grad_up, h_all, call))
         grad_down = contract_rows(h_all, call).astype(BF)
         inputs = tokens.astype(F32)
         inv_rms = inv[:, :1]
@@ -368,10 +391,10 @@
         ).astype(BF)
         grad_gain = jnp.sum(grad_normed * normal_rows, axis=0)
         for axis in ("depth", "col"):
-            bit = 1
-            while bit < mesh.shape[axis]:
-                grad_gain = swap_add(grad_gain, axis, bit)
-                bit *= 2
+            count = mesh.shape[axis]
+            grad_gain = grad_gain + sum(
+                lax.ppermute(grad_gain, axis, [(i, (i + step) % count) for i in range(count)])
+                for step in range(1, count))
         return output, grad_tokens, grad_gain, grad_gate, grad_up, grad_down
 
     return body

time: 184 us -> 193 us (1.049)
  waiting for transfers between devices: 13.7 us -> 20.7 us
  starting transfers between devices: 3.95 us -> 6.11 us
    reduce_scatter x2, waiting for transfers between devices: 7.41 us -> 17.4 us  [body(): lax.psum_scatter(value, 'col', scatter_dimension=0, tiled=True).astype(F32)]
    ppermute x5 -> x1, waiting for transfers between devices: 5.75 us -> 0.01 us  [swap_add(): lax.ppermute(value, axis, [(i, i ^ bit) for i in range(count)])]
    ppermute x0 -> x6, starting transfers between devices: none -> 4.56 us  [body(): lax.ppermute(grad_gain, axis, [(i, (i + step) % count) for i in range(cou...]
    ppermute x0 -> x6, waiting for transfers between devices: none -> 2.71 us  [body(): lax.ppermute(grad_gain, axis, [(i, (i + step) % count) for i in range(cou...]
    ppermute x5 -> x1, starting transfers between devices: 3.69 us -> 1.28 us  [swap_add(): lax.ppermute(value, axis, [(i, i ^ bit) for i in range(count)])]
  transfers between devices with their start and end apart: 7 -> 9, of which waited for: 4 -> 4; matrix products, arithmetic and copies ran while one was open for 23% -> 21% of each run, Pallas kernels for 0% -> 0%
where the time goes in v3:
time: 193 us
  Pallas kernels  110 us (57%)
  matrix products  37.8 us (20%)
  waiting for transfers between devices  20.7 us (11%)
  between operations  14.1 us (7%)
  starting transfers between devices  6.11 us (3%)
  other arithmetic  3.48 us (2%)
    pallas_call x1, Pallas kernels, exchange(): pl.pallas_call(functools.partial(exchange_kernel, n_col, chunks, size, fe...  110 us
    dot_general x3, matrix products, contract_rows(): lax.dot_general(left, right, (((0,), (0,)), ((), ())), preferred_element_...  37.8 us
    reduce_scatter x2, waiting for transfers between devices, body(): lax.psum_scatter(value, 'col', scatter_dimension=0, tiled=True).astype(F32)  17.4 us
    ppermute x6, starting transfers between devices, body(): lax.ppermute(grad_gain, axis, [(i, (i + step) % count) for i in range(cou...  4.56 us
  transfers between devices with their start and end apart: 9, of which 4 were waited for; matrix products, arithmetic and copies ran while one was open for 21% of the time, Pallas kernels for 0%

profile of v3, /device:TPU:0, one launch (start us, length us, event | category | flops | bytes accessed | tf_op | source)
XLA Modules:
  0.0 192.9 jit_solution(15615234462154482826)
XLA Ops:
  7.2 0.0 reduce-scatter.5.cloned.1.call-start
  7.2 109.8 %shard_map.109 = (bf16[128,2048]{1,0:T(8,128)(2,1)}, bf16[128,2048]{1,0:T(8,128)(2,1)}, f32[32,128]{1,0:T(8,128)}, bf16[4,128,2048]{2,1,0:T(8,128)(2,1)}, bf16[4...) custom-call(bf16[32,2048]{1,0:T(8,128)(2,1)} %tok_ref.1, ...), custom_call_target="tpu_custom_call" | custom-call | flops 11274289152 | bytes 55050240 | tf_op jit(solution)/shard_map/pallas_call | solution.py:330
  117.0 0.0 reduce-scatter.5.cloned.1.call-update
  117.1 0.2 reduce-scatter.3.cloned.1.call-start
  117.3 0.5 reduce-scatter.3.cloned.1.call-update
  117.8 0.8 slice_reduce_fusion
  118.7 0.0 copy-start.5
  118.7 13.4 %bitcast_convert_fusion.1 = bf16[2048,3584]{1,0:T(8,128)(2,1)} fusion(bf16[4,128,2048]{2,1,0:T(8,128)(2,1)} %get-tuple-element.22, bf16[4,128,3584]{2,1,0:T(8,128)(2,1)} %get-tuple-element.23), kind=kOutput, calls=%fused_computation.1 | convolution fusion | flops 7523532800 | bytes 20447232 | tf_op jit(solution)/shard_map/dot_general | solution.py:16
  132.1 0.0 copy-done.3
  132.1 0.0 copy-start.2
  132.1 11.2 %bitcast_convert_fusion = bf16[2048,3584]{1,0:T(8,128)(2,1)} fusion(bf16[4,128,2048]{2,1,0:T(8,128)(2,1)S(1)} %copy-done.5, bf16[4,128,3584]{2,1,0:T(8,128)(2,1)S(1)} %copy-done.3), kind=kOutput, calls=%fused_computation | convolution fusion | flops 7523532800 | bytes 20447232 | tf_op jit(solution)/shard_map/dot_general | solution.py:16
  143.3 0.9 convert_element_type.29
  144.3 17.4 %reduce-scatter.3.cloned.1.call-done = bf16[32,2048]{1,0:T(8,128)(2,1)} async-done(((bf16[128,2048]{1,0:T(8,128)(2,1)}), bf16[32,2048]{1,0:T(8,128)(2,1)}) %reduce-scatter.3.cloned.1.call-update) | async-done | bytes 131088 | tf_op jit(solution)/shard_map/reduce_scatter | solution.py:373
  161.7 0.9 convert_element_type.28
  162.7 0.2 fusion.8
  162.9 0.1 collective-permute-start.3
  162.9 1.5 collective-permute-start.2
  164.5 0.2 collective-permute-start.1
  164.6 1.3 collective-permute-start
  165.9 13.2 %convolution_convert_fusion = bf16[3584,2048]{1,0:T(8,128)(2,1)} fusion(bf16[512,3584]{1,0:T(8,128)(2,1)} %bitcast.19, bf16[512,2048]{1,0:T(8,128)(2,1)S(1)} %bitcast.20), kind=kOutput, calls=%fused_computation.2 | convolution fusion | flops 7523532800 | bytes 20447232 | tf_op jit(solution)/shard_map/dot_general | solution.py:16
  179.1 0.0 collective-permute-done
  179.1 0.0 collective-permute-done.3
  179.1 0.0 collective-permute-done.2
  179.1 0.0 collective-permute-done.1
  179.1 0.6 collective-permute-start.6
  179.7 0.3 collective-permute-start.5
  180.0 1.9 %collective-permute-start.4 = (f32[2048]{0:T(1024)S(1)}, f32[2048]{0:T(1024)S(1)}, u32[]{:S(2)}, u32[]{:S(2)}) collective-permute-start(f32[2048]{0:T(1024)S(1)} %add_add_fusion.1), channel_id=1, source_target_pairs={{0,4},{4,8},{8,12},{12,0},{1,5},{5,9},{9,13},{13,1},{2,6},{6,10},{... | collective-permute-start | bytes 24584 | tf_op jit(solution)/shard_map/ppermute | solution.py:396
  182.0 0.8 fusion.7
  182.7 0.1 collective-permute-done.6
  182.8 1.5 collective-permute-done.5
  184.3 1.1 collective-permute-done.4
  185.5 0.6 add_add_fusion
  (12 shorter events, 0.0 us)
Async XLA Ops:
  7.2 136.2 %reduce-scatter.5.cloned.1.call-start = ((), (), s32[]{:S(2)}) async-start(), calls=%async_computation.3 | async-start | bytes 655360 | tf_op jit(solution)/shard_map/reduce_scatter | solution.py:373
  117.1 44.6 %reduce-scatter.3.cloned.1.call-start = ((), (), s32[]{:S(2)}) async-start(), calls=%async_computation.2 | async-start | bytes 655360 | tf_op jit(solution)/shard_map/reduce_scatter | solution.py:373
  118.7 13.4 %copy-start.3 = (bf16[4,128,3584]{2,1,0:T(8,128)(2,1)S(1)}, bf16[4,128,3584]{2,1,0:T(8,128)(2,1)}, u32[]{:S(2)}) copy-start(bf16[4,128,3584]{2,1,0:T(8,128)(2,1)} %get-tuple-element.24) | copy-start | bytes 11010052
  118.7 13.4 %copy-start.5 = (bf16[4,128,2048]{2,1,0:T(8,128)(2,1)S(1)}, bf16[4,128,2048]{2,1,0:T(8,128)(2,1)}, u32[]{:S(2)}) copy-start(bf16[4,128,2048]{2,1,0:T(8,128)(2,1)} %get-tuple-element.22) | copy-start | bytes 6291460
  132.1 30.5 %copy-start = (bf16[32,2048]{1,0:T(8,128)(2,1)S(1)}, bf16[32,2048]{1,0:T(8,128)(2,1)}, u32[]{:S(2)}) copy-start(bf16[32,2048]{1,0:T(8,128)(2,1)} %tok_ref.1) | copy-start | bytes 393220
  132.1 30.5 %copy-start.2 = (f32[2048]{0:T(1024)S(1)}, f32[2048]{0:T(1024)}, u32[]{:S(2)}) copy-start(f32[2048]{0:T(1024)} %param.7) | copy-start | bytes 24580
  132.1 33.8 %copy-start.4 = (bf16[4,128,2048]{2,1,0:T(8,128)(2,1)S(1)}, bf16[4,128,2048]{2,1,0:T(8,128)(2,1)}, u32[]{:S(2)}) copy-start(bf16[4,128,2048]{2,1,0:T(8,128)(2,1)} %get-tuple-element.26) | copy-start | bytes 6291460
  162.9 16.2 %collective-permute-start.3 = (f32[2048]{0:T(1024)S(1)}, f32[2048]{0:T(1024)S(1)}, u32[]{:S(2)}, u32[]{:S(2)}) collective-permute-start(f32[2048]{0:T(1024)S(1)} %get-tuple-element.34), channel_id=1, source_target_pairs={{0,3},{1,0},{2,1},{3,2},{4,7},{5,4},{6,5},{7,6},{8,11},{9,8},{10,9... | collective-permute-start | bytes 24584 | tf_op jit(solution)/shard_map/ppermute | solution.py:396
  162.9 16.2 %collective-permute-start.2 = (f32[2048]{0:T(1024)S(1)}, f32[2048]{0:T(1024)S(1)}, u32[]{:S(2)}, u32[]{:S(2)}) collective-permute-start(f32[2048]{0:T(1024)S(1)} %get-tuple-element.34), channel_id=1, source_target_pairs={{0,2},{1,3},{2,0},{3,1},{4,6},{5,7},{6,4},{7,5},{8,10},{9,11},{10,... | collective-permute-start | bytes 24584 | tf_op jit(solution)/shard_map/ppermute | solution.py:396
  164.5 14.6 %collective-permute-start.1 = (f32[2048]{0:T(1024)S(1)}, f32[2048]{0:T(1024)S(1)}, u32[]{:S(2)}, u32[]{:S(2)}) collective-permute-start(f32[2048]{0:T(1024)S(1)} %get-tuple-element.34), channel_id=1, source_target_pairs={{0,1},{1,2},{2,3},{3,0},{4,5},{5,6},{6,7},{7,4},{8,9},{9,10},{10,1... | collective-permute-start | bytes 24584 | tf_op jit(solution)/shard_map/ppermute | solution.py:396
  164.6 17.3 %copy-start.1 = (bf16[32,2048]{1,0:T(8,128)(2,1)S(1)}, bf16[32,2048]{1,0:T(8,128)(2,1)}, u32[]{:S(2)}) copy-start(bf16[32,2048]{1,0:T(8,128)(2,1)} %cot_ref.1) | copy-start | bytes 393220
  164.6 14.4 %collective-permute-start = (f32[32,1]{0,1:T(1,128)S(1)}, f32[32,1]{0,1:T(1,128)S(1)}, u32[]{:S(2)}, u32[]{:S(2)}) collective-permute-start(f32[32,1]{0,1:T(1,128)S(1)} %bitcast.18), channel_id=1, source_target_pairs={{0,16},{16,0},{1,17},{17,1},{2,18},{18,2},{3,19},{19,3},{4,20},{20... | collective-permute-start | bytes 392 | tf_op jit(solution)/shard_map/ppermute | solution.py:366
  179.1 3.7 %collective-permute-start.6 = (f32[2048]{0:T(1024)S(1)}, f32[2048]{0:T(1024)S(1)}, u32[]{:S(2)}, u32[]{:S(2)}) collective-permute-start(f32[2048]{0:T(1024)S(1)} %add_add_fusion.1), channel_id=1, source_target_pairs={{0,12},{4,0},{8,4},{12,8},{1,13},{5,1},{9,5},{13,9},{2,14},{6,2},{... | collective-permute-start | bytes 24584 | tf_op jit(solution)/shard_map/ppermute | solution.py:396
  179.7 4.6 %collective-permute-start.5 = (f32[2048]{0:T(1024)S(1)}, f32[2048]{0:T(1024)S(1)}, u32[]{:S(2)}, u32[]{:S(2)}) collective-permute-start(f32[2048]{0:T(1024)S(1)} %add_add_fusion.1), channel_id=1, source_target_pairs={{0,8},{4,12},{8,0},{12,4},{1,9},{5,13},{9,1},{13,5},{2,10},{6,14},... | collective-permute-start | bytes 24584 | tf_op jit(solution)/shard_map/ppermute | solution.py:396
  180.0 5.4 %collective-permute-start.4 = (f32[2048]{0:T(1024)S(1)}, f32[2048]{0:T(1024)S(1)}, u32[]{:S(2)}, u32[]{:S(2)}) collective-permute-start(f32[2048]{0:T(1024)S(1)} %add_add_fusion.1), channel_id=1, source_target_pairs={{0,4},{4,8},{8,12},{12,0},{1,5},{5,9},{9,13},{13,1},{2,6},{6,10},{... | collective-permute-start | bytes 24584 | tf_op jit(solution)/shard_map/ppermute | solution.py:396
Sparse Core Ops, SparseCore 0:
  117.2 22.2 reduce-scatter.4
  141.8 19.9 reduce-scatter.2

commit v4 on v3

--- a/solution.py
+++ b/solution.py
@@ -153,6 +153,13 @@
     sq_copy = pltpu.make_async_remote_copy(sq_out, sq_in, sq_sem.at[0], sq_sem.at[1], device_id=x_peer, device_id_type=MESH)
     sq_copy.start()
 
+    def y_act(which, origin):
+        rows = pl.ds(pl.multiple_of(origin * block, block), block)
+        return pltpu.make_async_remote_copy(
+            both.at[which, me, rows, :], (nall, call)[which].at[dep, rows, :],
+            ay_send.at[which, origin], ay_recv.at[which, origin],
+            device_id=y_peer, device_id_type=MESH)
+
     def hop(which, step, way):
         origin = col - step if way == 0 else col + step
         target = col + 1 if way == 0 else col - 1
@@ -179,6 +186,7 @@
                 both.at[which, me, rows, :], both.at[which, me, rows, :],
                 ring_send.at[which, step, 0], ring_recv.at[which, step, 0],
                 device_id={"col": col - 1}, device_id_type=MESH).wait_recv()
+            y_act(which, col - 1 - step).start()
 
         @pl.when(col + 1 + step < n_col)
         def _():
@@ -187,13 +195,16 @@
                 both.at[which, me, rows, :], both.at[which, me, rows, :],
                 ring_send.at[which, step, 1], ring_recv.at[which, step, 1],
                 device_id={"col": col + 1}, device_id_type=MESH).wait_recv()
+            y_act(which, col + 1 + step).start()
 
     sends(1, 0, lambda copy: copy.start())
+    y_act(1, col).start()
     sq_copy.wait()
     inv = lax.rsqrt((sq_out[...] + sq_in[...]) / width + EPS)
     inv_ref[...] = inv
     both[0, me, own_rows, :] = (inputs * inv[:, :1] * gain_ref[...]).astype(BF)
     sends(0, 0, lambda copy: copy.start())
+    y_act(0, col).start()
     for step in range(n_col - 1):
         for which in (1, 0):
             arrive(which, step)
@@ -206,10 +217,6 @@
     def remote(src, dst, a, b, to):
         return pltpu.make_async_remote_copy(src, dst, a, b, device_id=to, device_id_type=MESH)
 
-    def y_act(which):
-        out = (nall, call)[which]
-        return remote(both.at[which, me], out.at[dep], ay_send.at[which], ay_recv.at[which], y_peer)
-
     def c_act(which):
         return remote(both.at[which, me], both.at[which, me], ac_send.at[which], ac_recv.at[which], c_peer)
 
@@ -222,7 +229,6 @@
 
     for which in (1, 0):
         c_act(which).start()
-        y_act(which).start()
     for which in (1, 0):
         c_act(which).wait()
         own_act(which).start()
@@ -264,7 +270,8 @@
     acc_m[...] = jnp.zeros_like(acc_m)
     acc_g[...] = jnp.zeros_like(acc_g)
     for which in (1, 0):
-        y_act(which).wait_recv()
+        for origin in range(n_col):
+            y_act(which, origin).wait_recv()
         act_forward(which).start()
 
     @pl.loop(0, chunks)
@@ -299,7 +306,8 @@
     end_copy(1).start()
     pass_on(chunks - 1)
     for which in (1, 0):
-        y_act(which).wait_send()
+        for origin in range(n_col):
+            y_act(which, origin).wait_send()
         own_act(which).wait()
         act_forward(which).wait()
     end_copy(0).wait()
@@ -348,7 +356,7 @@
             pltpu.VMEM((2, rows, feat), BF),
             pltpu.VMEM((2, rows, feat), BF),
             dma((chunks, 3)), dma((2,)), dma((2, n_col, 2)), dma((2, n_col, 2)), dma((chunks,)), dma((chunks,)),
-        ] + [dma((chunks, 3))] * 7 + [dma((2,))] * 9,
+        ] + [dma((chunks, 3))] * 7 + [dma((2, n_col))] * 2 + [dma((2,))] * 7,
         compiler_params=pltpu.CompilerParams(
             collective_id=0, has_side_effects=True, vmem_limit_bytes=62 * 1024 * 1024
         ),
@@ -377,8 +385,8 @@
             value.reshape(-1, value.shape[2]) for value in (nall, call, gg_all, gu_all, h_all))
         grad_gate = contract_rows(nall, gg_all).astype(BF)
         grad_up = contract_rows(nall, gu_all).astype(BF)
-        mixed, grad_normed, grad_gate, grad_up, h_all, call = lax.optimization_barrier(
-            (mixed, grad_normed, grad_gate, grad_up, h_all, call))
+        grad_normed, grad_gate, grad_up, h_all, call = lax.optimization_barrier(
+            (grad_normed, grad_gate, grad_up, h_all, call))
         grad_down = contract_rows(h_all, call).astype(BF)
         inputs = tokens.astype(F32)
         inv_rms = inv[:, :1]

time: 193 us -> 170 us (0.88)
  waiting for transfers between devices: 20.7 us -> 3.65 us
  Pallas kernels: 110 us -> 104 us
    reduce_scatter x2, waiting for transfers between devices: 17.4 us -> 0.01 us  [body(): lax.psum_scatter(value, 'col', scatter_dimension=0, tiled=True).astype(F32)]
    pallas_call x1, Pallas kernels: 110 us -> 104 us  [exchange(): pl.pallas_call(functools.partial(exchange_kernel, n_col, chunks, size, fe...]
  transfers between devices with their start and end apart: 9 -> 9, of which waited for: 4 -> 2; matrix products, arithmetic and copies ran while one was open for 21% -> 24% of each run, Pallas kernels for 0% -> 0%
where the time goes in v4:
time: 170 us; the launch traced here: 169 us
  Pallas kernels  104 us (61%)
  matrix products  37.8 us (22%)
  between operations  14.1 us (8%)
  starting transfers between devices  6.01 us (4%)
  waiting for transfers between devices  3.65 us (2%)
  other arithmetic  3.46 us (2%)
    pallas_call x1, Pallas kernels, exchange(): pl.pallas_call(functools.partial(exchange_kernel, n_col, chunks, size, fe...  104 us
    dot_general x3, matrix products, contract_rows(): lax.dot_general(left, right, (((0,), (0,)), ((), ())), preferred_element_...  37.8 us
    ppermute x6, starting transfers between devices, body(): lax.ppermute(grad_gain, axis, [(i, (i + step) % count) for i in range(cou...  5.16 us
  transfers between devices with their start and end apart: 9, of which 2 were waited for; matrix products, arithmetic and copies ran while one was open for 24% of the time, Pallas kernels for 0%

profile of v4, /device:TPU:0, one launch (start us, length us, event | category | flops | bytes accessed | tf_op | source)
XLA Modules:
  0.0 169.5 jit_solution(6540205553273714696)
XLA Ops:
  7.2 0.0 reduce-scatter.5.cloned.1.call-start
  7.2 103.6 %shard_map.109 = (bf16[128,2048]{1,0:T(8,128)(2,1)}, bf16[128,2048]{1,0:T(8,128)(2,1)}, f32[32,128]{1,0:T(8,128)}, bf16[4,128,2048]{2,1,0:T(8,128)(2,1)}, bf16[4...) custom-call(bf16[32,2048]{1,0:T(8,128)(2,1)} %tok_ref.1, ...), custom_call_target="tpu_custom_call" | custom-call | flops 11274289152 | bytes 55050240 | tf_op jit(solution)/shard_map/pallas_call | solution.py:338
  110.8 0.0 reduce-scatter.5.cloned.1.call-update
  110.8 0.2 reduce-scatter.3.cloned.1.call-start
  111.0 0.5 reduce-scatter.3.cloned.1.call-update
  111.6 0.8 slice_reduce_fusion
  112.4 0.0 copy-start.5
  112.4 13.4 %bitcast_convert_fusion.1 = bf16[2048,3584]{1,0:T(8,128)(2,1)} fusion(bf16[4,128,2048]{2,1,0:T(8,128)(2,1)} %get-tuple-element.22, bf16[4,128,3584]{2,1,0:T(8,128)(2,1)} %get-tuple-element.23), kind=kOutput, calls=%fused_computation.1 | convolution fusion | flops 7523532800 | bytes 20447232 | tf_op jit(solution)/shard_map/dot_general | solution.py:16
  125.8 0.0 copy-done.3
  125.8 0.0 copy-done.5
  125.8 0.0 copy-start.2
  125.9 11.2 %bitcast_convert_fusion = bf16[2048,3584]{1,0:T(8,128)(2,1)} fusion(bf16[4,128,2048]{2,1,0:T(8,128)(2,1)S(1)} %copy-done.5, bf16[4,128,3584]{2,1,0:T(8,128)(2,1)S(1)} %copy-done.3), kind=kOutput, calls=%fused_computation | convolution fusion | flops 7523532800 | bytes 20447232 | tf_op jit(solution)/shard_map/dot_general | solution.py:16
  137.1 0.9 convert_element_type.31
  138.0 0.2 fusion.8
  138.2 0.5 collective-permute-start.3
  138.8 1.5 collective-permute-start.2
  140.3 0.0 collective-permute-start.1
  140.3 0.6 collective-permute-start
  140.9 0.0 copy-done.4
  140.9 13.2 %convolution_convert_fusion = bf16[3584,2048]{1,0:T(8,128)(2,1)} fusion(bf16[512,3584]{1,0:T(8,128)(2,1)} %bitcast.19, bf16[512,2048]{1,0:T(8,128)(2,1)S(1)} %bitcast.20), kind=kOutput, calls=%fused_computation.2 | convolution fusion | flops 7523532800 | bytes 20447232 | tf_op jit(solution)/shard_map/dot_general | solution.py:16
  154.0 0.0 collective-permute-done
  154.0 0.0 collective-permute-done.3
  154.0 0.0 collective-permute-done.2
  154.1 0.0 collective-permute-done.1
  154.1 2.5 %collective-permute-start.6 = (f32[2048]{0:T(1024)S(1)}, f32[2048]{0:T(1024)S(1)}, u32[]{:S(2)}, u32[]{:S(2)}) collective-permute-start(f32[2048]{0:T(1024)S(1)} %add_add_fusion.1), channel_id=1, source_target_pairs={{0,12},{4,0},{8,4},{12,8},{1,13},{5,1},{9,5},{13,9},{2,14},{6,2},{... | collective-permute-start | bytes 24584 | tf_op jit(solution)/shard_map/ppermute | solution.py:404
  156.6 0.0 collective-permute-start.5
  156.6 0.6 collective-permute-start.4
  157.2 1.7 %fusion.7 = (bf16[32,2048]{1,0:T(8,128)(2,1)}, bf16[32,2048]{1,0:T(8,128)(2,1)}) fusion(bf16[32,2048]{1,0:T(8,128)(2,1)S(1)} %copy-done, bf16[32,2048]{1,0:T(8,128)(2,1)S(1)} %copy-done.1, f32[32,2048]{1,0:T(8,128)S(1)} %convert_element_type.31, f32[32]{0:T(128)S(1)} %multiply_bitcast_fusion, f32[2048]{0:T(1024)S(1)} %copy-done.2, ...), kind=kLoop, calls=%fused_computation.12 | loop fusion | flops 786432 | bytes 925952 | tf_op jit(solution)/shard_map/convert_element_type | solution.py:399
  158.9 0.0 collective-permute-done.6
  158.9 2.3 %collective-permute-done.5 = f32[2048]{0:T(1024)S(1)} collective-permute-done((f32[2048]{0:T(1024)S(1)}, f32[2048]{0:T(1024)S(1)}, u32[]{:S(2)}, u32[]{:S(2)}) %collective-permute-start.5) | collective-permute-done | bytes 8224 | tf_op jit(solution)/shard_map/ppermute | solution.py:404
  161.2 0.8 collective-permute-done.4
  162.0 0.6 add_add_fusion
  (11 shorter events, 0.0 us)
Async XLA Ops:
  7.2 129.9 %reduce-scatter.5.cloned.1.call-start = ((), (), s32[]{:S(2)}) async-start(), calls=%async_computation.3 | async-start | bytes 655360 | tf_op jit(solution)/shard_map/reduce_scatter | solution.py:381
  110.8 46.4 %reduce-scatter.3.cloned.1.call-start = ((), (), s32[]{:S(2)}) async-start(), calls=%async_computation.2 | async-start | bytes 655360 | tf_op jit(solution)/shard_map/reduce_scatter | solution.py:381
  112.4 13.4 %copy-start.3 = (bf16[4,128,3584]{2,1,0:T(8,128)(2,1)S(1)}, bf16[4,128,3584]{2,1,0:T(8,128)(2,1)}, u32[]{:S(2)}) copy-start(bf16[4,128,3584]{2,1,0:T(8,128)(2,1)} %get-tuple-element.24) | copy-start | bytes 11010052
  112.4 13.4 %copy-start.5 = (bf16[4,128,2048]{2,1,0:T(8,128)(2,1)S(1)}, bf16[4,128,2048]{2,1,0:T(8,128)(2,1)}, u32[]{:S(2)}) copy-start(bf16[4,128,2048]{2,1,0:T(8,128)(2,1)} %get-tuple-element.22) | copy-start | bytes 6291460
  125.8 12.2 %copy-start = (bf16[32,2048]{1,0:T(8,128)(2,1)S(1)}, bf16[32,2048]{1,0:T(8,128)(2,1)}, u32[]{:S(2)}) copy-start(bf16[32,2048]{1,0:T(8,128)(2,1)} %tok_ref.1) | copy-start | bytes 393220
  125.8 12.2 %copy-start.2 = (f32[2048]{0:T(1024)S(1)}, f32[2048]{0:T(1024)}, u32[]{:S(2)}) copy-start(f32[2048]{0:T(1024)} %param.7) | copy-start | bytes 24580
  125.9 15.0 %copy-start.4 = (bf16[4,128,2048]{2,1,0:T(8,128)(2,1)S(1)}, bf16[4,128,2048]{2,1,0:T(8,128)(2,1)}, u32[]{:S(2)}) copy-start(bf16[4,128,2048]{2,1,0:T(8,128)(2,1)} %get-tuple-element.26) | copy-start | bytes 6291460
  138.2 15.8 %collective-permute-start.3 = (f32[2048]{0:T(1024)S(1)}, f32[2048]{0:T(1024)S(1)}, u32[]{:S(2)}, u32[]{:S(2)}) collective-permute-start(f32[2048]{0:T(1024)S(1)} %get-tuple-element.32), channel_id=1, source_target_pairs={{0,3},{1,0},{2,1},{3,2},{4,7},{5,4},{6,5},{7,6},{8,11},{9,8},{10,9... | collective-permute-start | bytes 24584 | tf_op jit(solution)/shard_map/ppermute | solution.py:404
  138.8 15.3 %collective-permute-start.2 = (f32[2048]{0:T(1024)S(1)}, f32[2048]{0:T(1024)S(1)}, u32[]{:S(2)}, u32[]{:S(2)}) collective-permute-start(f32[2048]{0:T(1024)S(1)} %get-tuple-element.32), channel_id=1, source_target_pairs={{0,2},{1,3},{2,0},{3,1},{4,6},{5,7},{6,4},{7,5},{8,10},{9,11},{10,... | collective-permute-start | bytes 24584 | tf_op jit(solution)/shard_map/ppermute | solution.py:404
  140.3 13.8 %collective-permute-start.1 = (f32[2048]{0:T(1024)S(1)}, f32[2048]{0:T(1024)S(1)}, u32[]{:S(2)}, u32[]{:S(2)}) collective-permute-start(f32[2048]{0:T(1024)S(1)} %get-tuple-element.32), channel_id=1, source_target_pairs={{0,1},{1,2},{2,3},{3,0},{4,5},{5,6},{6,7},{7,4},{8,9},{9,10},{10,1... | collective-permute-start | bytes 24584 | tf_op jit(solution)/shard_map/ppermute | solution.py:404
  140.3 16.9 %copy-start.1 = (bf16[32,2048]{1,0:T(8,128)(2,1)S(1)}, bf16[32,2048]{1,0:T(8,128)(2,1)}, u32[]{:S(2)}) copy-start(bf16[32,2048]{1,0:T(8,128)(2,1)} %cot_ref.1) | copy-start | bytes 393220
  140.3 13.8 %collective-permute-start = (f32[32,1]{0,1:T(1,128)S(1)}, f32[32,1]{0,1:T(1,128)S(1)}, u32[]{:S(2)}, u32[]{:S(2)}) collective-permute-start(f32[32,1]{0,1:T(1,128)S(1)} %bitcast.18), channel_id=1, source_target_pairs={{0,16},{16,0},{1,17},{17,1},{2,18},{18,2},{3,19},{19,3},{4,20},{20... | collective-permute-start | bytes 392 | tf_op jit(solution)/shard_map/ppermute | solution.py:374
  154.1 4.8 %collective-permute-start.6 = (f32[2048]{0:T(1024)S(1)}, f32[2048]{0:T(1024)S(1)}, u32[]{:S(2)}, u32[]{:S(2)}) collective-permute-start(f32[2048]{0:T(1024)S(1)} %add_add_fusion.1), channel_id=1, source_target_pairs={{0,12},{4,0},{8,4},{12,8},{1,13},{5,1},{9,5},{13,9},{2,14},{6,2},{... | collective-permute-start | bytes 24584 | tf_op jit(solution)/shard_map/ppermute | solution.py:404
  156.6 4.6 %collective-permute-start.5 = (f32[2048]{0:T(1024)S(1)}, f32[2048]{0:T(1024)S(1)}, u32[]{:S(2)}, u32[]{:S(2)}) collective-permute-start(f32[2048]{0:T(1024)S(1)} %add_add_fusion.1), channel_id=1, source_target_pairs={{0,8},{4,12},{8,0},{12,4},{1,9},{5,13},{9,1},{13,5},{2,10},{6,14},... | collective-permute-start | bytes 24584 | tf_op jit(solution)/shard_map/ppermute | solution.py:404
  156.6 5.4 %collective-permute-start.4 = (f32[2048]{0:T(1024)S(1)}, f32[2048]{0:T(1024)S(1)}, u32[]{:S(2)}, u32[]{:S(2)}) collective-permute-start(f32[2048]{0:T(1024)S(1)} %add_add_fusion.1), channel_id=1, source_target_pairs={{0,4},{4,8},{8,12},{12,0},{1,5},{5,9},{9,13},{13,1},{2,6},{6,10},{... | collective-permute-start | bytes 24584 | tf_op jit(solution)/shard_map/ppermute | solution.py:404
Sparse Core Ops, SparseCore 0:
  110.9 19.8 reduce-scatter.4
  133.1 19.7 reduce-scatter.2
